TPU v7x, 256 devices: a whole 4x4x8 slice. The times are simulated.
256 devices in a mesh: head: 16 (over y, x), ctx: 16 (over z, core).
Axes of the slice: x: 4, y: 4, z: 8, core: 2. Of those that a mesh axis runs over, the one named last changes fastest.
Arguments:
- queries: bfloat16 [256, 128, 576], P('head'), may hold values from -41 to 41
- cache: bfloat16 [32768, 576], P('ctx'), may hold values from -11 to 11
- cache_len: int32 [16], P('ctx'), may hold values from 1 to 2048, 24576 in all
- span_start: int32 [1], replicated, may hold values from 28672 to 32512
- value_up: bfloat16 [128, 512, 128], P('head'), may hold values from -0.25 to 0.25
Outputs:
- attended: bfloat16 [256, 128, 128], P('ctx', 'head')
Inputs may be any that keep to these rules, and one draw needn't show every extreme that they name: Shard c holds cache_len[c] filled slots at its start; some shard is full.
All inputs are finite; a program needn't handle non-finite values.
Results may differ from a plain program's by a relative error of at most 0.01.
Values may be sent and summed in bfloat16 or wider, within the bound.
No kernel may reach another device: no remote copies, remote signals or barrier semaphores. Data moves between devices by JAX's collectives and lax.ppermute only.
A program may use at most 128 MiB of HBM per device.

v0:
```python
import jax
import jax.numpy as jnp
from jax import lax
from jax.sharding import PartitionSpec as P

DC = 512
DR = 64
NOPE = 128


def body(queries, cache, cache_len, span_start, value_up):
    local_q = lax.all_to_all(queries, "head", split_axis=1, concat_axis=0, tiled=True)
    tokens, heads, width = local_q.shape
    slot_count = cache.shape[0]
    shard = lax.axis_index("ctx")
    scale = (NOPE + DR) ** (-0.5)
    rows = local_q.reshape(tokens * heads, width)
    scores = jnp.dot(rows, cache.T, preferred_element_type=jnp.float32) * scale
    scores = scores.reshape(tokens, heads, slot_count)
    slots = jnp.arange(slot_count, dtype=jnp.int32)
    limit = span_start[0] + jnp.arange(tokens, dtype=jnp.int32)
    valid = (slots[None, :] < cache_len[0]) & (
        shard * slot_count + slots[None, :] <= limit[:, None]
    )
    mask = valid[:, None, :]
    shard_max = jnp.max(jnp.where(mask, scores, jnp.float32(-1e30)), axis=2, keepdims=True)
    weights = jnp.where(mask, jnp.exp(scores - shard_max), jnp.float32(0.0))
    total = jnp.sum(weights, axis=2)
    bounded = jnp.maximum(total, jnp.float32(1.0))
    flat = weights.astype(jnp.bfloat16).reshape(tokens * heads, slot_count)
    acc = jnp.dot(flat, cache[:, :DC], preferred_element_type=jnp.float32).reshape(
        tokens, heads, DC
    )
    partial_value = (acc / bounded[:, :, None]).astype(jnp.bfloat16)
    lse = shard_max[:, :, 0] + jnp.log(bounded)
    top = lax.pmax(lse, "ctx")
    scaled = jnp.exp(lse - top)
    numer, denom = (
        lax.psum_scatter(
            scaled[:, :, None] * partial_value.astype(jnp.float32),
            "ctx",
            scatter_dimension=0,
            tiled=True,
        ),
        lax.psum_scatter(scaled, "ctx", scatter_dimension=0, tiled=True),
    )
    merged = numer / denom[:, :, None]
    out = jnp.einsum(
        "shc,hcv->shv", merged, value_up.astype(jnp.float32), precision=lax.Precision.HIGHEST
    )
    return out.astype(jnp.bfloat16)


def solution(mesh):
    placed = (P("head", None, None), P("ctx", None), P("ctx"), P(), P("head", None, None))
    return jax.shard_map(
        body, mesh=mesh, in_specs=placed, out_specs=P("ctx", "head", None), check_vma=False
    )
```

profile of v0, /device:TPU:1, one launch (start us, length us, event | category | flops | bytes accessed | tf_op | source)
XLA Modules:
  0.0 257.8 jit_solution(474460065254979720)
XLA Ops:
  6.5 0.0 copy-start
  6.5 5.0 %copy.13 = bf16[16,128,576]{2,0,1:T(8,128)(2,1)} copy(bf16[16,128,576]{1,2,0:T(8,128)(2,1)} %param.5) | data formatting | bytes 4718592 | tf_op args[0]
  11.5 7.6 %all-to-all-start = ((bf16[16,128,576]{2,0,1:T(8,128)(2,1)}), bf16[16,128,576]{2,0,1:T(8,128)(2,1)}, u32[]{:S(2)}, u32[]{:S(2)}) async-start(bf16[16,128,576]{2,0,1:T(8,128)(2,1)} %copy.13), calls=%async_computation | async-start | bytes 5242880 | tf_op jit(solution)/shard_map/all_to_all | solution.py:12
  19.2 0.0 reduce-scatter.5.cloned.1.call-start
  20.5 0.4 compare_and_fusion
  21.0 37.2 %all-to-all-done = bf16[16,128,576]{2,0,1:T(8,128)(2,1)} async-done(((bf16[16,128,576]{2,0,1:T(8,128)(2,1)}), bf16[16,128,576]{2,0,1:T(8,128)(2,1)}, u32[]{:S(2)}, u32[]{:S(2)}) %all-to-all-start) | async-done | bytes 2359328 | tf_op jit(solution)/shard_map/all_to_all | solution.py:12
  58.1 0.0 copy-start.1
  58.1 2.5 copy.15
  60.7 0.0 copy-done.1
  60.7 11.5 %fusion = (f32[2048]{0:T(1024)S(1)}, f32[2048,2048]{1,0:T(8,128)}) fusion(pred[256,2048]{1,0:T(8,128)(4,1)S(1)} %compare_and_fusion, bf16[2048,576]{1,0:T(8,128)(2,1)S(1)} %bitcast.32, bf16[2048,576]{0,1:T(8,128)(2,1)S(1)} %copy-done.1), kind=kOutput, calls=%fused_computation.2 | convolution fusion | flops 4844419072 | bytes 22028288 | tf_op jit(solution)/shard_map/dot_general | solution.py:18
  72.2 0.1 reduce_max.12
  72.3 11.5 %fusion.3 = (bf16[256,8,2048]{2,1,0:T(8,128)(2,1)}, f32[2048]{0:T(1024)S(1)}) fusion(f32[2048,2048]{1,0:T(8,128)} %get-tuple-element.8, f32[2048]{0:T(1024)S(1)} %get-tuple-element.7, pred[256,2048]{1,0:T(8,128)(4,1)S(1)} %compare_and_fusion), kind=kLoop, calls=%fused_computation.5 | loop fusion | flops 20969472 | bytes 25706496 | tf_op jit(solution)/shard_map/dot_general | solution.py:31
  83.8 0.1 max.17
  83.9 0.1 copy.19
  84.0 48.8 %pmax.7 = f32[256,8]{1,0:T(8,128)S(1)} all-reduce(f32[256,8]{1,0:T(8,128)S(1)} %log_add_fusion), channel_id=1, replica_groups=mesh['head'=16,'ctx'=16] {'ctx'}, use_global_device_ids=true, to_apply=%region_2.3 | all-reduce | flops 2048 | bytes 16384 | tf_op jit(solution)/shard_map/pmax | solution.py:36
  132.8 0.7 subtract_exponential_fusion
  133.5 0.0 reduce-scatter.5.cloned.1.call-update
  133.5 0.2 reduce-scatter.3.cloned.1.call-start
  133.8 1.0 copy.16
  134.7 15.9 %convert_multiply_fusion = f32[256,8,512]{2,0,1:T(8,128)} fusion(f32[256,8]{0,1:T(8,128)S(1)} %copy.19, f32[256,8]{0,1:T(8,128)S(1)} %copy.16, bf16[2048,576]{0,1:T(8,128)(2,1)} %param.6, bf16[256,8,2048]{2,1,0:T(8,128)(2,1)} %get-tuple-element.5), kind=kOutput, calls=%fused_computation.8 | convolution fusion | flops 4299161600 | bytes 14696448 | tf_op jit(solution)/shard_map/dot_general | solution.py:31
  150.6 0.0 reduce-scatter.3.cloned.1.call-update
  150.7 34.3 %reduce-scatter.5.cloned.1.call-done = f32[16,8]{1,0:T(8,128)} async-done(((f32[256,8]{1,0:T(8,128)}), f32[16,8]{1,0:T(8,128)}) %reduce-scatter.5.cloned.1.call-update) | async-done | bytes 528 | tf_op jit(solution)/shard_map/reduce_scatter | solution.py:45
  185.0 0.8 copy.20
  185.7 63.0 %reduce-scatter.3.cloned.1.call-done = f32[16,8,512]{2,0,1:T(8,128)} async-done(((f32[256,8,512]{2,0,1:T(8,128)}), f32[16,8,512]{2,0,1:T(8,128)}) %reduce-scatter.3.cloned.1.call-update) | async-done | bytes 262160 | tf_op jit(solution)/shard_map/reduce_scatter | solution.py:39
  248.8 0.0 copy-done
  248.8 1.5 fusion.12
  250.3 0.6 copy.21
  (5 shorter events, 0.1 us)
Async XLA Ops:
  6.5 242.3 %copy-start = (bf16[8,512,128]{2,1,0:T(8,128)(2,1)S(1)}, bf16[8,512,128]{2,1,0:T(8,128)(2,1)}, u32[]{:S(2)}) copy-start(bf16[8,512,128]{2,1,0:T(8,128)(2,1)} %param.9) | copy-start | bytes 3145732
  11.5 46.6 %all-to-all-start = ((bf16[16,128,576]{2,0,1:T(8,128)(2,1)}), bf16[16,128,576]{2,0,1:T(8,128)(2,1)}, u32[]{:S(2)}, u32[]{:S(2)}) async-start(bf16[16,128,576]{2,0,1:T(8,128)(2,1)} %copy.13), calls=%async_computation | async-start | bytes 5242880 | tf_op jit(solution)/shard_map/all_to_all | solution.py:12
  19.2 165.8 %reduce-scatter.5.cloned.1.call-start = ((), (), s32[]{:S(2)}) async-start(), calls=%async_computation.4 | async-start | bytes 139264 | tf_op jit(solution)/shard_map/reduce_scatter | solution.py:45
  58.1 2.5 copy-start.1
  133.5 115.3 %reduce-scatter.3.cloned.1.call-start = ((), (), s32[]{:S(2)}) async-start(), calls=%async_computation.3 | async-start | bytes 4456448 | tf_op jit(solution)/shard_map/reduce_scatter | solution.py:39
Sparse Core Ops, SparseCore 0:
  133.6 51.2 reduce-scatter.4
  187.7 61.0 reduce-scatter.2
where the time goes:
time: 260 us; the launch traced here: 258 us
  waiting for transfers between devices  135 us (52%)
  blocking collectives  48.8 us (19%)
  matrix products  29 us (11%)
  between operations  14.8 us (6%)
  other arithmetic  12.6 us (5%)
  local copies, waits for them, and re-layouts  10.1 us (4%)
  starting transfers between devices  7.89 us (3%)
    reduce_scatter x1, waiting for transfers between devices, body(): lax.psum_scatter(scaled[:, :, None] * partial_value.astype(jnp.float32),...  63 us
    pmax x1, blocking collectives, body(): top = lax.pmax(lse, 'ctx')  48.8 us
    all_to_all x1, waiting for transfers between devices, body(): lax.all_to_all(queries, 'head', split_axis=1, concat_axis=0, tiled=True)  37.2 us
    reduce_scatter x1, waiting for transfers between devices, body(): lax.psum_scatter(scaled, 'ctx', scatter_dimension=0, tiled=True)  34.3 us
    dot_general x1, matrix products, body(): jnp.dot(flat, cache[:, :DC], preferred_element_type=jnp.float32)  15.9 us
    dot_general x1, matrix products, body(): scores = jnp.dot(rows, cache.T, preferred_element_type=jnp.float32) * scale  11.5 us
    dot_general x1, other arithmetic, body(): jnp.dot(flat, cache[:, :DC], preferred_element_type=jnp.float32)  11.5 us
    all_to_all x1, starting transfers between devices, body(): lax.all_to_all(queries, 'head', split_axis=1, concat_axis=0, tiled=True)  7.63 us
  transfers between devices with their start and end apart: 3, of which 3 were waited for; matrix products, arithmetic and copies ran while one was open for 7% of the time, Pallas kernels for 0%

commit v1 on v0

v1 whole, which is shorter than its diff:
```python
import math

import jax
import jax.numpy as jnp
from jax import lax
from jax.experimental import pallas as pl
from jax.experimental.pallas import tpu as pltpu
from jax.sharding import Mesh, PartitionSpec as P

DC = 512
DR = 64
NOPE = 128
DV = 128
WIDE = 640
HL = 4
TOK = 16
NH = 16
NZ = 8
SLOTS = 2048
ROWS = NH * TOK * HL
BLK = 512
NBLK = SLOTS // BLK
RC = 256
SCALE2 = (NOPE + DR) ** (-0.5) * math.log2(math.e)
LOW = -1e30
BF = jnp.bfloat16
F32 = jnp.float32
VM = pl.BlockSpec(memory_space=pltpu.VMEM)
SM = pl.BlockSpec(memory_space=pltpu.SMEM)
ANY = pl.BlockSpec(memory_space=pl.ANY)
HEAD = ("y", "x")
CTX = ("z", "core")


def dot(a, b):
    return jnp.dot(a, b, preferred_element_type=F32)


def pack_kernel(core_ref, q_ref, out_ref):
    core = core_ref[0]
    r = lax.broadcasted_iota(jnp.int32, (256, 512), 0)
    c = lax.broadcasted_iota(jnp.int32, (256, 512), 1)
    head = 8 * (r // 16) + 4 * core + r % 4
    pick = ((r // 4) % 4 == c // 128) & (head == c % 128)
    pick = jnp.where(pick, 1.0, 0.0).astype(BF)
    rot = []
    for t in range(4):
        x = jnp.concatenate([q_ref[4 * t + i] for i in range(4)], axis=1)
        y = lax.dot_general(pick, x, (((1,), (1,)), ((), ())), preferred_element_type=F32).astype(BF)
        for j in range(4):
            out_ref[:, 64 * j + 16 * t : 64 * j + 16 * t + 16, :] = y[:, 128 * j : 128 * j + 128].reshape(16, 16, 128)
        rot.append(y[:, DC:])
    for t in range(2):
        out_ref[:, 256 + 16 * t : 272 + 16 * t, :] = jnp.concatenate([rot[t], rot[t + 2]], axis=1).reshape(16, 16, 128)


def pack(core, q):
    return pl.pallas_call(
        pack_kernel,
        out_shape=jax.ShapeDtypeStruct((NH, 288, 128), BF),
        in_specs=[SM, VM],
        out_specs=VM,
        compiler_params=pltpu.CompilerParams(vmem_limit_bytes=24 * 2**20),
        cost_estimate=pl.CostEstimate(flops=10**9, bytes_accessed=4 * 10**6, transcendentals=0),
    )(core, q)


def turn_kernel(c_ref, out_ref):
    x = c_ref[...]
    out_ref[...] = jnp.concatenate([x, x[DC:]], axis=0).T


def turn(c):
    return pl.pallas_call(
        turn_kernel,
        grid=(NBLK,),
        out_shape=jax.ShapeDtypeStruct((SLOTS, WIDE), BF),
        in_specs=[pl.BlockSpec((DC + DR, BLK), lambda i: (0, i))],
        out_specs=pl.BlockSpec((BLK, WIDE), lambda i: (i, 0)),
        compiler_params=pltpu.CompilerParams(vmem_limit_bytes=24 * 2**20),
        cost_estimate=pl.CostEstimate(flops=10**9, bytes_accessed=5 * 10**6, transcendentals=0),
    )(c)


def attend_kernel(sc_ref, q_ref, w_ref, k0, k1, v0, v1, out_ref, k_scr, v_scr, qt, acc, ml, sem):
    core = sc_ref[0]
    span = sc_ref[1]
    ks, vs = (k0, k1), (v0, v1)
    bases = [sc_ref[4 + s] * SLOTS for s in range(2)]
    many = []
    for s in range(2):
        reach = jnp.clip(span + 256 - bases[s], 0, SLOTS)
        many.append((jnp.minimum(sc_ref[2 + s], reach) + BLK - 1) // BLK)

    def copies(s, i):
        lo = i * BLK
        if not isinstance(i, int):
            lo = pl.multiple_of(lo, BLK)
        return (
            pltpu.make_async_copy(ks[s].at[pl.ds(lo, BLK), :], k_scr.at[s, i], sem.at[0, s, i]),
            pltpu.make_async_copy(vs[s].at[pl.ds(0, DC), pl.ds(lo, BLK)], v_scr.at[s, i], sem.at[1, s, i]),
        )

    for s in range(2):
        for i in range(NBLK):

            @pl.when(i < many[s])
            def _():
                for c in copies(s, i):
                    c.start()

    acc[...] = jnp.zeros_like(acc)
    ml[0:1] = jnp.full((1, ROWS), LOW, F32)
    ml[1:2] = jnp.zeros((1, ROWS), F32)
    for j in range(4):
        qt[128 * j : 128 * j + 128, :] = q_ref[:, 64 * j : 64 * j + 64, :].reshape(ROWS, 128).T
    rot = q_ref[:, 256:288, :]
    lane = lax.broadcasted_iota(jnp.int32, rot.shape, 2)
    nil = jnp.zeros_like(rot)
    rot = jnp.concatenate([jnp.where(lane < 64, rot, nil), jnp.where(lane < 64, nil, rot)], axis=1)
    qt[DC:WIDE, :] = rot.reshape(ROWS, 128).T

    slot = lax.broadcasted_iota(jnp.int32, (BLK, RC), 0)
    for s in range(2):

        def block(i, _, s=s):
            for c in copies(s, i):
                c.wait()
            kb, vb = k_scr[s, i], v_scr[s, i]
            for rc in range(ROWS // RC):
                cols = slice(RC * rc, RC * rc + RC)
                token = (lax.broadcasted_iota(jnp.int32, (1, RC), 1) + RC * rc) // HL
                limit = jnp.minimum(sc_ref[2 + s], span + 1 + token - bases[s]) - i * BLK
                sco = dot(kb, qt[:, cols])
                sco = jnp.where(slot < limit, sco, LOW)
                old = ml[0:1, cols]
                new = jnp.maximum(old, jnp.max(sco, axis=0, keepdims=True))
                p = jnp.exp2((sco - new) * SCALE2)
                shrink = jnp.exp2((old - new) * SCALE2)
                ml[0:1, cols] = new
                ml[1:2, cols] = ml[1:2, cols] * shrink + jnp.sum(p, axis=0, keepdims=True)
                acc[:, cols] = acc[:, cols] * shrink + dot(vb, p.astype(BF))
            return 0

        lax.fori_loop(0, many[s], block, 0)

    for rc in range(ROWS // RC):
        cols = slice(RC * rc, RC * rc + RC)
        total = jnp.maximum(ml[1:2, cols], 1.0)
        lse = ml[0:1, cols] * SCALE2 + jnp.log2(total)
        part = (acc[:, cols] / total).astype(BF)
        up = dot(w_ref[...], part)
        which = lax.broadcasted_iota(jnp.int32, (1, RC), 1) % HL
        res = jnp.zeros((DV, RC), F32)
        for h in range(HL):
            res = jnp.where(which == h, up[DV * h : DV * h + DV], res)
        hi = lse.astype(BF)
        rest = lse - hi.astype(F32)
        mid = rest.astype(BF)
        low = (rest - mid.astype(F32)).astype(BF)
        row = lax.broadcasted_iota(jnp.int32, (16, RC), 0)
        tail = jnp.where(row == 0, hi.astype(F32), jnp.where(row == 1, mid.astype(F32), low.astype(F32)))
        res, tail = res.astype(BF), tail.astype(BF)
        for u in range(RC // 128):
            z = rc * (RC // 128) + u
            out_ref[z, 0:DV, :] = res[:, 128 * u : 128 * u + 128]
            out_ref[z, DV : DV + 16, :] = tail[:, 128 * u : 128 * u + 128]


def attend(sc, q, w, k0, k1, v0, v1):
    return pl.pallas_call(
        attend_kernel,
        out_shape=jax.ShapeDtypeStruct((NZ, DV + 16, 128), BF),
        in_specs=[SM, VM, VM, ANY, ANY, ANY, ANY],
        out_specs=VM,
        scratch_shapes=[
            pltpu.VMEM((2, NBLK, BLK, WIDE), BF),
            pltpu.VMEM((2, NBLK, DC, BLK), BF),
            pltpu.VMEM((WIDE, ROWS), BF),
            pltpu.VMEM((DC, ROWS), F32),
            pltpu.VMEM((8, ROWS), F32),
            pltpu.SemaphoreType.DMA((2, 2, NBLK)),
        ],
        compiler_params=pltpu.CompilerParams(vmem_limit_bytes=40 * 2**20),
        cost_estimate=pl.CostEstimate(flops=10**10, bytes_accessed=12 * 10**6, transcendentals=4 * 10**6),
    )(sc, q, w, k0, k1, v0, v1)


def merge_kernel(core_ref, x_ref, keep_ref, send_ref, scr):
    core = core_ref[0]
    lses = []
    for z in range(NZ):
        t = x_ref[z, DV : DV + 16, :].astype(F32)
        lses.append(t[0:1] + t[1:2] + t[2:3])
    top = lses[0]
    for z in range(1, NZ):
        top = jnp.maximum(top, lses[z])
    num = jnp.zeros((DV, 128), F32)
    den = jnp.zeros((1, 128), F32)
    for z in range(NZ):
        wz = jnp.exp2(lses[z] - top)
        den = den + wz
        num = num + wz * x_ref[z, 0:DV, :].astype(F32)
    out = (num / den).T
    scr[0] = out[:64]
    scr[1] = out[64:]
    keep_ref[...] = scr[core].astype(BF)
    send_ref[...] = scr[1 - core].astype(BF)


def merge(core, x):
    return pl.pallas_call(
        merge_kernel,
        out_shape=(jax.ShapeDtypeStruct((64, 128), BF), jax.ShapeDtypeStruct((64, 128), BF)),
        in_specs=[SM, VM],
        out_specs=(VM, VM),
        scratch_shapes=[pltpu.VMEM((2, 64, 128), F32)],
        cost_estimate=pl.CostEstimate(flops=10**6, bytes_accessed=3 * 10**5, transcendentals=1000),
    )(core, x)


def body(queries, cache, cache_len, span_start, value_up):
    core = lax.axis_index("core")
    shard = lax.axis_index(CTX)
    swap = [(0, 1), (1, 0)]
    core_a = core.reshape(1).astype(jnp.int32)
    packed = pack(core_a, queries.transpose(0, 2, 1))
    q = lax.all_to_all(packed, HEAD, split_axis=0, concat_axis=0, tiled=True)
    mine = cache.T
    other = lax.ppermute(mine, "core", swap)
    other_len = lax.ppermute(cache_len, "core", swap)
    k0, k1 = turn(mine), turn(other)
    w = lax.dynamic_slice_in_dim(value_up, HL * core, HL, 0).transpose(0, 2, 1).reshape(HL * DV, DC)
    sc = jnp.stack([core, span_start[0], cache_len[0], other_len[0], shard, shard + 1 - 2 * core, 0, 0]).astype(jnp.int32)
    part = attend(sc, q, w, k0, k1, mine, other)
    parts = lax.all_to_all(part, "z", split_axis=0, concat_axis=0, tiled=True)
    keep, send = merge(core_a, parts)
    got = lax.ppermute(send, "core", swap)
    keep, got = keep.reshape(TOK, HL, DV), got.reshape(TOK, HL, DV)
    first = jnp.where(core == 0, keep, got)
    second = jnp.where(core == 0, got, keep)
    return jnp.concatenate([first, second], axis=1)


def solution(mesh):
    fine = Mesh(mesh.devices.reshape(4, 4, 8, 2), ("y", "x", "z", "core"))
    placed = (P(HEAD, None, None), P(CTX, None), P(CTX), P(), P(HEAD, None, None))
    return jax.shard_map(body, mesh=fine, in_specs=placed, out_specs=P(CTX, HEAD, None), check_vma=False)
```

time: 260 us -> 95.6 us (0.37)
  waiting for transfers between devices: 135 us -> 7.98 us
  Pallas kernels: 0 us -> 37.5 us
  blocking collectives: 48.8 us -> 19.7 us
  matrix products: 29 us -> 0 us
  between operations: 14.8 us -> 1.39 us
  other arithmetic: 12.6 us -> 1.36 us
  starting transfers between devices: 7.89 us -> 12.2 us
  local copies, waits for them, and re-layouts: 10.1 us -> 13.9 us
    reduce_scatter x2 -> x0, waiting for transfers between devices: 97.3 us -> none  [the longest x1 63 us: body(): lax.psum_scatter(scaled[:, :, None] * partial_value.astype(jnp.float32),...]
    pmax x1 -> x0, blocking collectives: 48.8 us -> none  [body(): top = lax.pmax(lse, 'ctx')]
    pallas_call x0 -> x5, Pallas kernels: none -> 37.5 us  [the longest x1 30.7 us: attend(): pl.pallas_call(attend_kernel, out_shape=jax.ShapeDtypeStruct((NZ, DV + 16...]
    all_to_all x1, waiting for transfers between devices: 37.2 us -> 6.92 us  [body(): q = lax.all_to_all(packed, HEAD, split_axis=0, concat_axis=0, tiled=True)]
    dot_general x3 -> x0, matrix products: 29 us -> none  [the longest x1 15.9 us: body(): jnp.dot(flat, cache[:, :DC], preferred_element_type=jnp.float32)]
    all_to_all x0 -> x1, blocking collectives: none -> 19.7 us  [body(): parts = lax.all_to_all(part, 'z', split_axis=0, concat_axis=0, tiled=True)]
    dot_general x1 -> x0, other arithmetic: 11.5 us -> none  [body(): jnp.dot(flat, cache[:, :DC], preferred_element_type=jnp.float32)]
    ppermute x0 -> x3, starting transfers between devices: none -> 7.01 us  [the longest x1 3.32 us: body(): got = lax.ppermute(send, 'core', swap)]
  transfers between devices with their start and end apart: 3 -> 4, of which waited for: 3 -> 2; matrix products, arithmetic and copies ran while one was open for 7% -> 4% of each run, Pallas kernels for 0% -> 5%
where the time goes in v1:
time: 95.6 us; the launch traced here: 94 us
  Pallas kernels  37.5 us (39%)
  blocking collectives  19.7 us (21%)
  local copies, waits for them, and re-layouts  13.9 us (15%)
  starting transfers between devices  12.2 us (13%)
  waiting for transfers between devices  7.98 us (8%)
  between operations  1.39 us (1%)
  other arithmetic  1.36 us (1%)
    pallas_call x1, Pallas kernels, attend(): pl.pallas_call(attend_kernel, out_shape=jax.ShapeDtypeStruct((NZ, DV + 16...  30.7 us
    all_to_all x1, blocking collectives, body(): parts = lax.all_to_all(part, 'z', split_axis=0, concat_axis=0, tiled=True)  19.7 us
    unnamed x18, local copies, waits for them, and re-layouts  10.2 us
    all_to_all x1, waiting for transfers between devices, body(): q = lax.all_to_all(packed, HEAD, split_axis=0, concat_axis=0, tiled=True)  6.92 us
    all_to_all x1, starting transfers between devices, body(): q = lax.all_to_all(packed, HEAD, split_axis=0, concat_axis=0, tiled=True)  5.21 us
    pallas_call x2, Pallas kernels, turn(): pl.pallas_call(turn_kernel, grid=(NBLK,), out_shape=jax.ShapeDtypeStruct(...  3.99 us
    ppermute x1, starting transfers between devices, body(): got = lax.ppermute(send, 'core', swap)  3.32 us
    ppermute x1, starting transfers between devices, body(): other = lax.ppermute(mine, 'core', swap)  3.24 us
  transfers between devices with their start and end apart: 4, of which 2 were waited for; matrix products, arithmetic and copies ran while one was open for 4% of the time, Pallas kernels for 5%

profile of v1, /device:TPU:1, one launch (start us, length us, event | category | flops | bytes accessed | tf_op | source)
XLA Modules:
  0.0 94.0 jit_solution(5183930836495542578)
XLA Ops:
  0.0 0.0 copy-start
  0.0 3.2 %collective-permute-start.1 = (bf16[576,2048]{1,0:T(8,128)(2,1)}, bf16[576,2048]{1,0:T(8,128)(2,1)}, u32[]{:S(2)}, u32[]{:S(2)}) collective-permute-start(bf16[576,2048]{1,0:T(8,128)(2,1)} %bitcast.10), channel_id=1, source_target_pairs={{0,1},{1,0},{2,3},{3,2},{4,5},{5,4},{6,7},{7,6},{8,9},{9,8},{10,11... | collective-permute-start | bytes 7077896 | tf_op jit(solution)/shard_map/ppermute | solution.py:230
  3.2 0.0 copy-start.8
  3.2 1.7 %copy-done.8 = bf16[16,128,576]{1,2,0:T(8,128)(2,1)S(1)} copy-done((bf16[16,128,576]{1,2,0:T(8,128)(2,1)S(1)}, bf16[16,128,576]{1,2,0:T(8,128)(2,1)}, u32[]{:S(2)}) %copy-start.8) | copy-done | bytes 2359320
  4.9 1.1 %shard_map.55 = bf16[16,288,128]{2,1,0:T(8,128)(2,1)S(1)} custom-call(s32[1]{0:T(128)} %bitcast.core_ref, bf16[16,576,128]{2,1,0:T(8,128)(2,1)S(1)} %bitcast.14), custom_call_target="tpu_custom_call" | custom-call | flops 1000000000 | bytes 4000000 | tf_op jit(solution)/shard_map/pallas_call | solution.py:58
  6.0 1.0 %copy-done.6 = bf16[16,288,128]{2,1,0:T(8,128)(2,1)} copy-done((bf16[16,288,128]{2,1,0:T(8,128)(2,1)}, bf16[16,288,128]{2,1,0:T(8,128)(2,1)S(1)}, u32[]{:S(2)}) %copy-start.6) | copy-done | bytes 1179672
  7.0 5.2 %all-to-all-start = ((bf16[16,288,128]{2,1,0:T(8,128)(2,1)}), bf16[16,288,128]{2,1,0:T(8,128)(2,1)}, u32[]{:S(2)}, u32[]{:S(2)}) async-start(bf16[16,288,128]{2,1,0:T(8,128)(2,1)} %copy-done.6), calls=%async_computation | async-start | bytes 2359296 | tf_op jit(solution)/shard_map/all_to_all | solution.py:228
  12.3 0.4 collective-permute-start
  14.0 0.0 copy-done
  14.0 0.8 dynamic-slice_bitcast_fusion
  14.9 2.1 %copy.6 = bf16[4,128,512]{2,1,0:T(8,128)(2,1)} copy(bf16[4,128,512]{1,2,0:T(8,128)(2,1)} %dynamic-slice_bitcast_fusion) | data formatting | bytes 1048576 | tf_op jit(solution)/shard_map/transpose | solution.py:233
  16.9 0.0 copy-done.5
  16.9 1.1 %shard_map.56.k0 = bf16[2048,640]{1,0:T(8,128)(2,1)S(1)} custom-call(bf16[576,2048]{1,0:T(8,128)(2,1)S(1)} %bitcast.11), custom_call_target="tpu_custom_call" | custom-call | flops 1000000000 | bytes 5000000 | tf_op jit(solution)/shard_map/pallas_call | solution.py:74
  18.0 0.0 copy-start.1
  18.1 1.5 %copy-done.1 = bf16[2048,640]{1,0:T(8,128)(2,1)} copy-done((bf16[2048,640]{1,0:T(8,128)(2,1)}, bf16[2048,640]{1,0:T(8,128)(2,1)S(1)}, u32[]{:S(2)}) %copy-start.1) | copy-done | bytes 2621464
  19.5 0.0 collective-permute-done
  19.5 0.8 stack.12.sc_ref
  20.3 0.0 collective-permute-done.1.c_ref.v1
  20.3 2.9 %shard_map.57.k1 = bf16[2048,640]{1,0:T(8,128)(2,1)S(1)} custom-call(bf16[576,2048]{1,0:T(8,128)(2,1)} %collective-permute-done.1.c_ref.v1), custom_call_target="tpu_custom_call" | custom-call | flops 1000000000 | bytes 5000000 | tf_op jit(solution)/shard_map/pallas_call | solution.py:74
  23.2 0.0 copy-start.3
  23.2 1.5 %copy-done.3 = bf16[2048,640]{1,0:T(8,128)(2,1)} copy-done((bf16[2048,640]{1,0:T(8,128)(2,1)}, bf16[2048,640]{1,0:T(8,128)(2,1)S(1)}, u32[]{:S(2)}) %copy-start.3) | copy-done | bytes 2621464
  24.7 6.9 %all-to-all-done.q_ref = bf16[16,288,128]{2,1,0:T(8,128)(2,1)} async-done(((bf16[16,288,128]{2,1,0:T(8,128)(2,1)}), bf16[16,288,128]{2,1,0:T(8,128)(2,1)}, u32[]{:S(2)}, u32[]{:S(2)}) %all-to-all-start) | async-done | bytes 1179680 | tf_op jit(solution)/shard_map/all_to_all | solution.py:228
  31.6 1.7 %copy-done.2 = bf16[2048,640]{1,0:T(8,128)(2,1)S(1)} copy-done((bf16[2048,640]{1,0:T(8,128)(2,1)S(1)}, bf16[2048,640]{1,0:T(8,128)(2,1)}, u32[]{:S(2)}) %copy-start.2) | copy-done | bytes 2621464
  33.4 1.7 %copy-done.4 = bf16[2048,640]{1,0:T(8,128)(2,1)S(1)} copy-done((bf16[2048,640]{1,0:T(8,128)(2,1)S(1)}, bf16[2048,640]{1,0:T(8,128)(2,1)}, u32[]{:S(2)}) %copy-start.4) | copy-done | bytes 2621464
  35.1 1.0 %copy-done.7 = bf16[4,128,512]{2,1,0:T(8,128)(2,1)S(1)} copy-done((bf16[4,128,512]{2,1,0:T(8,128)(2,1)S(1)}, bf16[4,128,512]{2,1,0:T(8,128)(2,1)}, u32[]{:S(2)}) %copy-start.7) | copy-done | bytes 524312
  36.2 30.7 %shard_map.58 = bf16[8,144,128]{2,1,0:T(8,128)(2,1)S(1)} custom-call(s32[8]{0:T(128)S(1)} %stack.12.sc_ref, bf16[16,288,128]{2,1,0:T(8,128)(2,1)} %all-to-all-done.q_ref, bf16[512,512]{1,0:T(8,128)(2,1)S(1)} %bitcast.13, bf16[2048,640]{1,0:T(8,128)(2,1)S(1)} %copy-done.2, bf16[2048,640]{1,0:T(8,128)(2,1)S(1)} %copy-done.4, bf16[576,2048]{1,0:T(8,128)(2,1)S(1)} %bitcast.12, ...), custom_call_target="tpu_custom_call" | custom-call | flops 10000000000 | bytes 12000000 | tf_op jit(solution)/shard_map/pallas_call | solution.py:171
  66.8 19.7 %all_to_all.10.x_ref = bf16[8,144,128]{2,1,0:T(8,128)(2,1)} all-to-all(bf16[8,144,128]{2,1,0:T(8,128)(2,1)S(1)} %shard_map.58), channel_id=1, replica_groups=mesh['y'=4,'x'=4,'z'=8,'core'=2] {'z'}, dimensions={0} | all-to-all | bytes 589824 | tf_op jit(solution)/shard_map/all_to_all | solution.py:236
  86.5 1.7 %shard_map.59 = (bf16[64,128]{1,0:T(8,128)(2,1)}, bf16[64,128]{1,0:T(8,128)(2,1)}) custom-call(s32[1]{0:T(128)} %bitcast.core_ref, bf16[8,144,128]{2,1,0:T(8,128)(2,1)} %all_to_all.10.x_ref), custom_call_target="tpu_custom_call" | custom-call | flops 1000000 | bytes 300000 | tf_op jit(solution)/shard_map/pallas_call | solution.py:212
  88.3 3.3 %collective-permute-start.2 = (bf16[64,128]{1,0:T(8,128)(2,1)}, bf16[64,128]{1,0:T(8,128)(2,1)S(1)}, u32[]{:S(2)}, u32[]{:S(2)}) collective-permute-start(bf16[64,128]{1,0:T(8,128)(2,1)} %get-tuple-element.8), channel_id=1, source_target_pairs={{0,1},{1,0},{2,3},{3,2},{4,5},{5,4},{6,7},{7,6},{8,9},{9,8},{10,11... | collective-permute-start | bytes 49160 | tf_op jit(solution)/shard_map/ppermute | solution.py:238
  91.6 1.0 %collective-permute-done.2 = bf16[64,128]{1,0:T(8,128)(2,1)S(1)} collective-permute-done((bf16[64,128]{1,0:T(8,128)(2,1)}, bf16[64,128]{1,0:T(8,128)(2,1)S(1)}, u32[]{:S(2)}, u32[]{:S(2)}) %collective-permute-start.2) | collective-permute-done | bytes 16416 | tf_op jit(solution)/shard_map/ppermute | solution.py:238
  92.6 0.7 broadcast_select_fusion.1
  93.4 0.6 pad_maximum_fusion
  (6 shorter events, 0.0 us)
Async XLA Ops:
  0.0 14.0 %copy-start = (bf16[8,512,128]{2,1,0:T(8,128)(2,1)S(1)}, bf16[8,512,128]{2,1,0:T(8,128)(2,1)}, u32[]{:S(2)}) copy-start(bf16[8,512,128]{2,1,0:T(8,128)(2,1)} %param.9) | copy-start | bytes 3145732
  0.0 20.3 %collective-permute-start.1 = (bf16[576,2048]{1,0:T(8,128)(2,1)}, bf16[576,2048]{1,0:T(8,128)(2,1)}, u32[]{:S(2)}, u32[]{:S(2)}) collective-permute-start(bf16[576,2048]{1,0:T(8,128)(2,1)} %bitcast.10), channel_id=1, source_target_pairs={{0,1},{1,0},{2,3},{3,2},{4,5},{5,4},{6,7},{7,6},{8,9},{9,8},{10,11... | collective-permute-start | bytes 7077896 | tf_op jit(solution)/shard_map/ppermute | solution.py:230
  3.2 1.7 %copy-start.8 = (bf16[16,128,576]{1,2,0:T(8,128)(2,1)S(1)}, bf16[16,128,576]{1,2,0:T(8,128)(2,1)}, u32[]{:S(2)}) copy-start(bf16[16,128,576]{1,2,0:T(8,128)(2,1)} %param.5) | copy-start | bytes 7077892
  6.0 1.0 %copy-start.6 = (bf16[16,288,128]{2,1,0:T(8,128)(2,1)}, bf16[16,288,128]{2,1,0:T(8,128)(2,1)S(1)}, u32[]{:S(2)}) copy-start(bf16[16,288,128]{2,1,0:T(8,128)(2,1)S(1)} %shard_map.55) | copy-start | bytes 3538948
  7.0 9.9 %copy-start.5 = (bf16[2048,576]{0,1:T(8,128)(2,1)S(1)}, bf16[2048,576]{0,1:T(8,128)(2,1)}, u32[]{:S(2)}) copy-start(bf16[2048,576]{0,1:T(8,128)(2,1)} %param.6) | copy-start | bytes 7077892
  7.0 24.6 %all-to-all-start = ((bf16[16,288,128]{2,1,0:T(8,128)(2,1)}), bf16[16,288,128]{2,1,0:T(8,128)(2,1)}, u32[]{:S(2)}, u32[]{:S(2)}) async-start(bf16[16,288,128]{2,1,0:T(8,128)(2,1)} %copy-done.6), calls=%async_computation | async-start | bytes 2359296 | tf_op jit(solution)/shard_map/all_to_all | solution.py:228
  12.3 7.3 %collective-permute-start = (s32[1]{0:T(128)}, s32[1]{0:T(128)}, u32[]{:S(2)}, u32[]{:S(2)}) collective-permute-start(s32[1]{0:T(128)} %param.7), channel_id=1, source_target_pairs={{0,1},{1,0},{2,3},{3,2},{4,5},{5,4},{6,7},{7,6},{8,9},{9,8},{10,11... | collective-permute-start | bytes 20 | tf_op jit(solution)/shard_map/ppermute | solution.py:231
  18.0 1.5 %copy-start.1 = (bf16[2048,640]{1,0:T(8,128)(2,1)}, bf16[2048,640]{1,0:T(8,128)(2,1)S(1)}, u32[]{:S(2)}) copy-start(bf16[2048,640]{1,0:T(8,128)(2,1)S(1)} %shard_map.56.k0) | copy-start | bytes 7864324
  23.2 1.5 %copy-start.3 = (bf16[2048,640]{1,0:T(8,128)(2,1)}, bf16[2048,640]{1,0:T(8,128)(2,1)S(1)}, u32[]{:S(2)}) copy-start(bf16[2048,640]{1,0:T(8,128)(2,1)S(1)} %shard_map.57.k1) | copy-start | bytes 7864324
  31.6 1.7 %copy-start.2 = (bf16[2048,640]{1,0:T(8,128)(2,1)S(1)}, bf16[2048,640]{1,0:T(8,128)(2,1)}, u32[]{:S(2)}) copy-start(bf16[2048,640]{1,0:T(8,128)(2,1)} %copy-done.1) | copy-start | bytes 7864324
  33.4 1.7 %copy-start.4 = (bf16[2048,640]{1,0:T(8,128)(2,1)S(1)}, bf16[2048,640]{1,0:T(8,128)(2,1)}, u32[]{:S(2)}) copy-start(bf16[2048,640]{1,0:T(8,128)(2,1)} %copy-done.3) | copy-start | bytes 7864324
  35.1 1.0 %copy-start.7 = (bf16[4,128,512]{2,1,0:T(8,128)(2,1)S(1)}, bf16[4,128,512]{2,1,0:T(8,128)(2,1)}, u32[]{:S(2)}) copy-start(bf16[4,128,512]{2,1,0:T(8,128)(2,1)} %copy.6) | copy-start | bytes 1572868
  88.3 4.4 %collective-permute-start.2 = (bf16[64,128]{1,0:T(8,128)(2,1)}, bf16[64,128]{1,0:T(8,128)(2,1)S(1)}, u32[]{:S(2)}, u32[]{:S(2)}) collective-permute-start(bf16[64,128]{1,0:T(8,128)(2,1)} %get-tuple-element.8), channel_id=1, source_target_pairs={{0,1},{1,0},{2,3},{3,2},{4,5},{5,4},{6,7},{7,6},{8,9},{9,8},{10,11... | collective-permute-start | bytes 49160 | tf_op jit(solution)/shard_map/ppermute | solution.py:238

commit v2 on v0

v2 whole, which is shorter than its diff:
```python
import functools
import math

import jax
import jax.numpy as jnp
from jax import lax
from jax.experimental import pallas as pl
from jax.experimental.pallas import tpu as pltpu
from jax.sharding import Mesh, PartitionSpec as P

DC = 512
DR = 64
NOPE = 128
DV = 128
WIDE = 640
HL = 4
NC = 1
HC = HL // NC
TOK = 16
TG = 16 // HC
NG = TOK // TG
CR = TOK * HC
QR = CR * 9 // 2
NH = 16
NX = 16
SLOTS = 2048
ROWS = NH * CR
BLK = 1024
NBLK = SLOTS // BLK
SCALE2 = (NOPE + DR) ** (-0.5) * math.log2(math.e)
LOW = -1e30
BF = jnp.bfloat16
F32 = jnp.float32
VM = pl.BlockSpec(memory_space=pltpu.VMEM)
SM = pl.BlockSpec(memory_space=pltpu.SMEM)
ANY = pl.BlockSpec(memory_space=pl.ANY)
HEAD = ("y", "x")
CTX = ("z", "core")
BIG = 60 * 2**20


def dot(a, b):
    return jnp.dot(a, b, preferred_element_type=F32)


def iota(shape, dim):
    return lax.broadcasted_iota(jnp.int32, shape, dim)


def pack_kernel(chunk, core_ref, q_ref, out_ref, q_scr, o_scr, sem, osem):
    loads = [pltpu.make_async_copy(q_ref.at[t], q_scr.at[t], sem.at[t]) for t in range(TOK)]
    for c in loads:
        c.start()
    core = core_ref[0]
    shape = (NH * 16, TG * 128)
    r, c = iota(shape, 0), iota(shape, 1)
    head = 8 * (r // 16) + HL * core + HC * chunk + r % HC
    pick = ((r // HC) % TG == c // 128) & (head == c % 128)
    pick = jnp.where(pick, 1.0, 0.0).astype(BF)
    rot = []
    for t in range(NG):
        for i in range(TG):
            loads[TG * t + i].wait()
        x = jnp.concatenate([q_scr[TG * t + i] for i in range(TG)], axis=1)
        y = lax.dot_general(pick, x, (((1,), (1,)), ((), ())), preferred_element_type=F32).astype(BF)
        for j in range(4):
            o_scr[:, CR * j + 16 * t : CR * j + 16 * t + 16, :] = y[:, 128 * j : 128 * j + 128].reshape(NH, 16, 128)
        rot.append(y[:, DC:])
    for t in range(NG // 2):
        pair = jnp.concatenate([rot[t], rot[t + NG // 2]], axis=1)
        o_scr[:, 4 * CR + 16 * t : 4 * CR + 16 * t + 16, :] = pair.reshape(NH, 16, 128)
    stores = [pltpu.make_async_copy(o_scr.at[g], out_ref.at[g], osem.at[g]) for g in range(NH)]
    for c in stores:
        c.start()
    for c in stores:
        c.wait()


def pack(core, q, chunk):
    return pl.pallas_call(
        functools.partial(pack_kernel, chunk),
        out_shape=jax.ShapeDtypeStruct((NH, QR, 128), BF),
        in_specs=[SM, ANY],
        out_specs=ANY,
        scratch_shapes=[
            pltpu.VMEM((TOK, DC + DR, 128), BF),
            pltpu.VMEM((NH, QR, 128), BF),
            pltpu.SemaphoreType.DMA((TOK,)),
            pltpu.SemaphoreType.DMA((NH,)),
        ],
        compiler_params=pltpu.CompilerParams(vmem_limit_bytes=BIG),
        cost_estimate=pl.CostEstimate(flops=10**9, bytes_accessed=4 * 10**6, transcendentals=0),
    )(core, q)


def turn_kernel(c_ref, out_ref):
    x = c_ref[...]
    out_ref[...] = jnp.concatenate([x, x[DC:]], axis=0).T


def turn(c):
    return pl.pallas_call(
        turn_kernel,
        grid=(4,),
        out_shape=jax.ShapeDtypeStruct((SLOTS, WIDE), BF),
        in_specs=[pl.BlockSpec((DC + DR, SLOTS // 4), lambda i: (0, i))],
        out_specs=pl.BlockSpec((SLOTS // 4, WIDE), lambda i: (i, 0)),
        compiler_params=pltpu.CompilerParams(vmem_limit_bytes=BIG),
        cost_estimate=pl.CostEstimate(flops=10**9, bytes_accessed=5 * 10**6, transcendentals=0),
    )(c)


def attend_kernel(sc_ref, q_ref, w_ref, k0, k1, v0, v1, out_ref, q_scr, w_scr, k_scr, v_scr, qt, sco, acc, ml, sem):
    span = sc_ref[1]
    ks, vs = (k0, k1), (v0, v1)
    qcopy = pltpu.make_async_copy(q_ref, q_scr, sem.at[2, 0])
    wcopy = pltpu.make_async_copy(w_ref, w_scr, sem.at[2, 1])
    kcopy, vcopy = [], []
    for b in range(2 * NBLK):
        at = pl.ds(b % NBLK * BLK, BLK)
        kcopy.append(pltpu.make_async_copy(ks[b // NBLK].at[at, :], k_scr.at[b], sem.at[0, b]))
        vcopy.append(pltpu.make_async_copy(vs[b // NBLK].at[pl.ds(0, DC), at], v_scr.at[b], sem.at[1, b]))
    qcopy.start()
    for c in kcopy:
        c.start()
    for c in vcopy:
        c.start()
    wcopy.start()

    qcopy.wait()
    for j in range(4):
        qt[128 * j : 128 * j + 128, :] = q_scr[:, CR * j : CR * j + CR, :].reshape(ROWS, 128).T
    rot = q_scr[:, 4 * CR :, :]
    lane = iota(rot.shape, 2)
    nil = jnp.zeros_like(rot)
    rot = jnp.concatenate([jnp.where(lane < 64, rot, nil), jnp.where(lane < 64, nil, rot)], axis=1)
    qt[DC:WIDE, :] = rot.reshape(ROWS, 128).T

    token = iota((1, ROWS), 1) // HC
    slot = iota((BLK, ROWS), 0)
    top = jnp.full((1, ROWS), LOW, F32)
    for b in range(2 * NBLK):
        s = b // NBLK
        limit = jnp.minimum(sc_ref[2 + s], span + 1 + token - sc_ref[4 + s] * SLOTS) - b % NBLK * BLK
        kcopy[b].wait()
        x = jnp.where(slot < limit, dot(k_scr[b], qt[...]), LOW)
        sco[b] = x
        top = jnp.maximum(top, jnp.max(x, axis=0, keepdims=True))
    ml[0:1] = top

    total = jnp.zeros((1, ROWS), F32)
    for b in range(2 * NBLK):
        vcopy[b].wait()
        p = jnp.exp2((sco[b] - ml[0:1]) * SCALE2)
        total = total + jnp.sum(p, axis=0, keepdims=True)
        up = dot(v_scr[b], p.astype(BF))
        acc[...] = up if b == 0 else acc[...] + up

    wcopy.wait()
    total = jnp.maximum(total, 1.0)
    lse = ml[0:1] * SCALE2 + jnp.log2(total)
    up = dot(w_scr[...], (acc[...] / total).astype(BF))
    which = iota((1, ROWS), 1) % HC
    res = up[0:DV]
    for h in range(1, HC):
        res = jnp.where(which == h, up[DV * h : DV * h + DV], res)
    out_ref[:, 0:CR, :] = res.T.astype(BF).reshape(NH, CR, DV)
    hi = lse.astype(BF).astype(F32)
    mid = (lse - hi).astype(BF).astype(F32)
    low = lse - hi - mid
    row = iota((16, ROWS), 0)
    tail = jnp.where(row == 0, hi, jnp.where(row == 1, mid, low)).astype(BF)
    for a in range(NX):
        line = a * CR // 128 * 128
        out_ref[a, CR : CR + 16, :] = tail[:, line : line + 128]


def attend(sc, q, w, k0, k1, v0, v1):
    return pl.pallas_call(
        attend_kernel,
        out_shape=jax.ShapeDtypeStruct((NX, CR + 16, 128), BF),
        in_specs=[SM, ANY, ANY, ANY, ANY, ANY, ANY],
        out_specs=VM,
        scratch_shapes=[
            pltpu.VMEM((NH, QR, 128), BF),
            pltpu.VMEM((HC * DV, DC), BF),
            pltpu.VMEM((2 * NBLK, BLK, WIDE), BF),
            pltpu.VMEM((2 * NBLK, DC, BLK), BF),
            pltpu.VMEM((WIDE, ROWS), BF),
            pltpu.VMEM((2 * NBLK, BLK, ROWS), F32),
            pltpu.VMEM((DC, ROWS), F32),
            pltpu.VMEM((8, ROWS), F32),
            pltpu.SemaphoreType.DMA((3, max(2 * NBLK, 2))),
        ],
        compiler_params=pltpu.CompilerParams(vmem_limit_bytes=BIG),
        cost_estimate=pl.CostEstimate(flops=10**10, bytes_accessed=12 * 10**6, transcendentals=4 * 10**6),
    )(sc, q, w, k0, k1, v0, v1)


def merge_kernel(sc_ref, *refs):
    xs, out_ref, scr = refs[:NC], refs[NC], refs[NC + 1]
    lines = []
    for x in xs:
        for k in range(2):
            lse = []
            for z in range(NX // 2):
                t = x[2 * z + k, CR : CR + 16, :].astype(F32)
                lse.append(t[0:1] + t[1:2] + t[2:3])
            lse = jnp.concatenate(lse, axis=0)
            wz = jnp.exp2(lse - jnp.max(lse, axis=0, keepdims=True))
            lines.append(wz / jnp.sum(wz, axis=0, keepdims=True))
    lines.append(jnp.zeros((128 - 16 * NC, 128), F32))
    scr[...] = jnp.concatenate(lines, axis=0).T
    off = sc_ref[6] % (128 // CR) * CR
    wt = scr[pl.ds(pl.multiple_of(off, CR), CR), :]
    merged = []
    for c, x in enumerate(xs):
        for k in range(2):
            num = jnp.zeros((CR, DV), F32)
            for z in range(NX // 2):
                at = c * NX + k * (NX // 2) + z
                num = num + wt[:, at : at + 1] * x[2 * z + k, 0:CR, :].astype(F32)
            merged.append(num.astype(BF))
    merged = jnp.concatenate(merged, axis=0)
    r, c = iota((128, 128), 0), iota((128, 128), 1)
    head = HL * (c // CR % 2) + HC * (c // (2 * CR)) + c % HC
    pick = (r // 8 == c % CR // HC) & (r % 8 == head)
    out_ref[...] = dot(jnp.where(pick, 1.0, 0.0).astype(BF), merged).astype(BF)


def merge(sc, xs):
    return pl.pallas_call(
        merge_kernel,
        out_shape=jax.ShapeDtypeStruct((TOK * 2 * HL, DV), BF),
        in_specs=[SM] + [VM] * NC,
        out_specs=VM,
        scratch_shapes=[pltpu.VMEM((128, 128), F32)],
        cost_estimate=pl.CostEstimate(flops=10**6, bytes_accessed=3 * 10**5, transcendentals=1000),
    )(sc, *xs)


def body(queries, cache, cache_len, span_start, value_up):
    core = lax.axis_index("core")
    shard = lax.axis_index(CTX)
    swap = [(0, 1), (1, 0)]
    core_a = core.reshape(1).astype(jnp.int32)
    turned = queries.transpose(0, 2, 1)
    q = [
        lax.all_to_all(pack(core_a, turned, c), HEAD, split_axis=0, concat_axis=0, tiled=True) for c in range(NC)
    ]
    mine = cache.T
    other = lax.ppermute(mine, "core", swap)
    other_len = lax.ppermute(cache_len, "core", swap)
    k0, k1 = turn(mine), turn(other)
    sc = jnp.stack([core, span_start[0], cache_len[0], other_len[0], shard, shard + 1 - 2 * core, shard, 0]).astype(jnp.int32)
    parts = []
    for c in range(NC):
        w = lax.dynamic_slice_in_dim(value_up, HL * core + HC * c, HC, 0).transpose(0, 2, 1).reshape(HC * DV, DC)
        part = attend(sc, q[c], w, k0, k1, mine, other)
        parts.append(lax.all_to_all(part, CTX, split_axis=0, concat_axis=0, tiled=True))
    return merge(sc, parts).reshape(TOK, 2 * HL, DV)


def solution(mesh):
    fine = Mesh(mesh.devices.reshape(4, 4, 8, 2), ("y", "x", "z", "core"))
    placed = (P(HEAD, None, None), P(CTX, None), P(CTX), P(), P(HEAD, None, None))
    return jax.shard_map(body, mesh=fine, in_specs=placed, out_specs=P(CTX, HEAD, None), check_vma=False)
```

time: 260 us -> 74.4 us (0.29)
  waiting for transfers between devices: 135 us -> 3.28 us
  Pallas kernels: 0 us -> 31.6 us
  matrix products: 29 us -> 0 us
  blocking collectives: 48.8 us -> 23.2 us
  between operations: 14.8 us -> 1.35 us
  other arithmetic: 12.6 us -> 0 us
  local copies, waits for them, and re-layouts: 10.1 us -> 5.55 us
    reduce_scatter x2 -> x0, waiting for transfers between devices: 97.3 us -> none  [the longest x1 63 us: body(): lax.psum_scatter(scaled[:, :, None] * partial_value.astype(jnp.float32),...]
    pmax x1 -> x0, blocking collectives: 48.8 us -> none  [body(): top = lax.pmax(lse, 'ctx')]
    all_to_all x1, waiting for transfers between devices: 37.2 us -> 3.27 us  [body(): lax.all_to_all(pack(core_a, turned, c), HEAD, split_axis=0, concat_axis=0...]
    pallas_call x0 -> x5, Pallas kernels: none -> 31.6 us  [the longest x1 16.4 us: attend(): pl.pallas_call(attend_kernel, out_shape=jax.ShapeDtypeStruct((NX, CR + 16...]
    dot_general x3 -> x0, matrix products: 29 us -> none  [the longest x1 15.9 us: body(): jnp.dot(flat, cache[:, :DC], preferred_element_type=jnp.float32)]
    all_to_all x0 -> x1, blocking collectives: none -> 23.2 us  [body(): lax.all_to_all(part, CTX, split_axis=0, concat_axis=0, tiled=True)]
    dot_general x1 -> x0, other arithmetic: 11.5 us -> none  [body(): jnp.dot(flat, cache[:, :DC], preferred_element_type=jnp.float32)]
    ppermute x0 -> x2, starting transfers between devices: none -> 3.87 us  [the longest x1 3.24 us: body(): other = lax.ppermute(mine, 'core', swap)]
  transfers between devices with their start and end apart: 3 -> 3, of which waited for: 3 -> 1; matrix products, arithmetic and copies ran while one was open for 7% -> 6% of each run, Pallas kernels for 0% -> 18%
where the time goes in v2:
time: 74.4 us; the launch traced here: 73.9 us
  Pallas kernels  31.6 us (42%)
  blocking collectives  23.2 us (31%)
  starting transfers between devices  8.96 us (12%)
  local copies, waits for them, and re-layouts  5.55 us (7%)
  waiting for transfers between devices  3.28 us (4%)
  between operations  1.35 us (2%)
    all_to_all x1, blocking collectives, body(): lax.all_to_all(part, CTX, split_axis=0, concat_axis=0, tiled=True)  23.2 us
    pallas_call x1, Pallas kernels, attend(): pl.pallas_call(attend_kernel, out_shape=jax.ShapeDtypeStruct((NX, CR + 16...  16.4 us
    pallas_call x2, Pallas kernels, turn(): pl.pallas_call(turn_kernel, grid=(4,), out_shape=jax.ShapeDtypeStruct((SL...  8.6 us
    all_to_all x1, starting transfers between devices, body(): lax.all_to_all(pack(core_a, turned, c), HEAD, split_axis=0, concat_axis=0...  5.09 us
    pallas_call x1, Pallas kernels, pack(): pl.pallas_call(functools.partial(pack_kernel, chunk), out_shape=jax.Shape...  4.44 us
    all_to_all x1, waiting for transfers between devices, body(): lax.all_to_all(pack(core_a, turned, c), HEAD, split_axis=0, concat_axis=0...  3.27 us
    ppermute x1, starting transfers between devices, body(): other = lax.ppermute(mine, 'core', swap)  3.24 us
    transpose x2, local copies, waits for them, and re-layouts, body(): lax.dynamic_slice_in_dim(value_up, HL * core + HC * c, HC, 0)  2.85 us
  transfers between devices with their start and end apart: 3, of which 1 were waited for; matrix products, arithmetic and copies ran while one was open for 6% of the time, Pallas kernels for 18%

profile of v2, /device:TPU:1, one launch (start us, length us, event | category | flops | bytes accessed | tf_op | source)
XLA Modules:
  0.0 73.9 jit_solution(7331839284182616821)
XLA Ops:
  0.0 0.0 copy-start
  0.0 3.2 %collective-permute-start.1 = (bf16[576,2048]{1,0:T(8,128)(2,1)}, bf16[576,2048]{1,0:T(8,128)(2,1)S(1)}, u32[]{:S(2)}, u32[]{:S(2)}) collective-permute-start(bf16[576,2048]{1,0:T(8,128)(2,1)} %bitcast.9), channel_id=1, source_target_pairs={{0,1},{1,0},{2,3},{3,2},{4,5},{5,4},{6,7},{7,6},{8,9},{9,8},{10,11... | collective-permute-start | bytes 7077896 | tf_op jit(solution)/shard_map/ppermute | solution.py:252
  3.2 4.4 %shard_map.55 = bf16[16,288,128]{2,1,0:T(8,128)(2,1)} custom-call(s32[1]{0:T(128)} %bitcast.core_ref, bf16[16,576,128]{2,1,0:T(8,128)(2,1)} %bitcast.13), custom_call_target="tpu_custom_call" | custom-call | flops 1000000000 | bytes 4000000 | tf_op jit(solution)/shard_map/pallas_call | solution.py:80
  7.7 5.1 %all-to-all-start = ((bf16[16,288,128]{2,1,0:T(8,128)(2,1)}), bf16[16,288,128]{2,1,0:T(8,128)(2,1)}, u32[]{:S(2)}, u32[]{:S(2)}) async-start(bf16[16,288,128]{2,1,0:T(8,128)(2,1)} %shard_map.55), calls=%async_computation | async-start | bytes 2359296 | tf_op jit(solution)/shard_map/all_to_all | solution.py:249
  12.8 0.6 collective-permute-start
  14.7 0.0 copy-done
  14.7 0.8 %dynamic-slice_bitcast_fusion = bf16[4,128,512]{1,2,0:T(8,128)(2,1)} fusion(bf16[8,512,128]{2,1,0:T(8,128)(2,1)S(1)} %copy-done, s32[]{:T(128)S(6)} %select_n.3), kind=kLoop, calls=%fused_computation | loop fusion | bytes 1048580 | tf_op jit(solution)/shard_map/transpose | solution.py:258
  15.6 2.0 %copy.6 = bf16[4,128,512]{2,1,0:T(8,128)(2,1)} copy(bf16[4,128,512]{1,2,0:T(8,128)(2,1)} %dynamic-slice_bitcast_fusion) | data formatting | bytes 1048576 | tf_op jit(solution)/shard_map/transpose | solution.py:258
  17.6 4.3 %shard_map.56.k0 = bf16[2048,640]{1,0:T(8,128)(2,1)} custom-call(bf16[576,2048]{1,0:T(8,128)(2,1)} %bitcast.10), custom_call_target="tpu_custom_call" | custom-call | flops 1000000000 | bytes 5000000 | tf_op jit(solution)/shard_map/pallas_call | solution.py:102
  21.9 0.0 collective-permute-done
  21.9 1.2 %stack.16.sc_ref = s32[8]{0:T(128)} concatenate(s32[1]{0:T(128)} %bitcast.core_ref, s32[1]{0:T(128)S(6)} %copy.8, s32[1]{0:T(128)S(6)} %copy.7, s32[1]{0:T(128)} %collective-permute-done, s32[1]{0:T(128)} %bitcast.1, s32[1]{0:T(128)} %bitcast.2, s32[1]{0:T(128)} %bitcast.1, s32[1]{0:T(128)} %constant.6.clone.1), dimensions={0} | concatenate | bytes 64 | tf_op jit(solution)/shard_map/stack | solution.py:255
  23.1 0.0 collective-permute-done.1.c_ref.v1
  23.1 0.0 copy-start.1
  23.1 1.5 %copy-done.1 = bf16[576,2048]{1,0:T(8,128)(2,1)} copy-done((bf16[576,2048]{1,0:T(8,128)(2,1)}, bf16[576,2048]{1,0:T(8,128)(2,1)S(1)}, u32[]{:S(2)}) %copy-start.1) | copy-done | bytes 2359320
  24.6 4.3 %shard_map.57.k1 = bf16[2048,640]{1,0:T(8,128)(2,1)} custom-call(bf16[576,2048]{1,0:T(8,128)(2,1)} %copy-done.1), custom_call_target="tpu_custom_call" | custom-call | flops 1000000000 | bytes 5000000 | tf_op jit(solution)/shard_map/pallas_call | solution.py:102
  28.9 3.3 %all-to-all-done.q_ref = bf16[16,288,128]{2,1,0:T(8,128)(2,1)} async-done(((bf16[16,288,128]{2,1,0:T(8,128)(2,1)}), bf16[16,288,128]{2,1,0:T(8,128)(2,1)}, u32[]{:S(2)}, u32[]{:S(2)}) %all-to-all-start) | async-done | bytes 1179680 | tf_op jit(solution)/shard_map/all_to_all | solution.py:249
  32.2 16.4 %shard_map.58 = bf16[16,80,128]{2,1,0:T(8,128)(2,1)} custom-call(s32[8]{0:T(128)} %stack.16.sc_ref, bf16[16,288,128]{2,1,0:T(8,128)(2,1)} %all-to-all-done.q_ref, bf16[512,512]{1,0:T(8,128)(2,1)} %bitcast.12, bf16[2048,640]{1,0:T(8,128)(2,1)} %shard_map.56.k0, bf16[2048,640]{1,0:T(8,128)(2,1)} %shard_map.57.k1, bf16[576,2048]{1,0:T(8,128)(2,1)} %bitcast.11, ...), custom_call_target="tpu_custom_call" | custom-call | flops 10000000000 | bytes 12000000 | tf_op jit(solution)/shard_map/pallas_call | solution.py:179
  48.5 23.2 %all_to_all.10.refs_0_ = bf16[16,80,128]{2,1,0:T(8,128)(2,1)} all-to-all(bf16[16,80,128]{2,1,0:T(8,128)(2,1)} %shard_map.58), channel_id=1, replica_groups=mesh['y'=4,'x'=4,'z'=8,'core'=2] {'z','core'}, dimensions={0} | all-to-all | bytes 655360 | tf_op jit(solution)/shard_map/all_to_all | solution.py:260
  71.7 2.2 %shard_map.59 = bf16[128,128]{1,0:T(8,128)(2,1)} custom-call(s32[8]{0:T(128)} %stack.16.sc_ref, bf16[16,80,128]{2,1,0:T(8,128)(2,1)} %all_to_all.10.refs_0_), custom_call_target="tpu_custom_call" | custom-call | flops 1000000 | bytes 300000 | tf_op jit(solution)/shard_map/pallas_call | solution.py:232
Async XLA Ops:
  0.0 14.7 %copy-start = (bf16[8,512,128]{2,1,0:T(8,128)(2,1)S(1)}, bf16[8,512,128]{2,1,0:T(8,128)(2,1)}, u32[]{:S(2)}) copy-start(bf16[8,512,128]{2,1,0:T(8,128)(2,1)} %param.9) | copy-start | bytes 3145732
  0.0 23.1 %collective-permute-start.1 = (bf16[576,2048]{1,0:T(8,128)(2,1)}, bf16[576,2048]{1,0:T(8,128)(2,1)S(1)}, u32[]{:S(2)}, u32[]{:S(2)}) collective-permute-start(bf16[576,2048]{1,0:T(8,128)(2,1)} %bitcast.9), channel_id=1, source_target_pairs={{0,1},{1,0},{2,3},{3,2},{4,5},{5,4},{6,7},{7,6},{8,9},{9,8},{10,11... | collective-permute-start | bytes 7077896 | tf_op jit(solution)/shard_map/ppermute | solution.py:252
  7.7 24.5 %all-to-all-start = ((bf16[16,288,128]{2,1,0:T(8,128)(2,1)}), bf16[16,288,128]{2,1,0:T(8,128)(2,1)}, u32[]{:S(2)}, u32[]{:S(2)}) async-start(bf16[16,288,128]{2,1,0:T(8,128)(2,1)} %shard_map.55), calls=%async_computation | async-start | bytes 2359296 | tf_op jit(solution)/shard_map/all_to_all | solution.py:249
  12.8 9.1 %collective-permute-start = (s32[1]{0:T(128)}, s32[1]{0:T(128)}, u32[]{:S(2)}, u32[]{:S(2)}) collective-permute-start(s32[1]{0:T(128)} %param.7), channel_id=1, source_target_pairs={{0,1},{1,0},{2,3},{3,2},{4,5},{5,4},{6,7},{7,6},{8,9},{9,8},{10,11... | collective-permute-start | bytes 20 | tf_op jit(solution)/shard_map/ppermute | solution.py:253
  23.1 1.5 %copy-start.1 = (bf16[576,2048]{1,0:T(8,128)(2,1)}, bf16[576,2048]{1,0:T(8,128)(2,1)S(1)}, u32[]{:S(2)}) copy-start(bf16[576,2048]{1,0:T(8,128)(2,1)S(1)} %collective-permute-done.1.c_ref.v1) | copy-start | bytes 7077892

commit v3 on v0

v3 whole, which is shorter than its diff:
```python
import math

import jax
import jax.numpy as jnp
from jax import lax
from jax.experimental import pallas as pl
from jax.experimental.pallas import tpu as pltpu
from jax.sharding import Mesh, PartitionSpec as P

DC = 512
DR = 64
NOPE = 128
DV = 128
WIDE = DC + DR
HL = 4
TOK = 16
TG = 16 // HL
CR = TOK * HL
QR = CR * 9 // 2
NH = 16
NX = 16
SLOTS = 2048
ROWS = NH * CR
BLK = 1024
NBLK = SLOTS // BLK
SCALE2 = (NOPE + DR) ** (-0.5) * math.log2(math.e)
LOW = -1e30
BF = jnp.bfloat16
F32 = jnp.float32
VM = pl.BlockSpec(memory_space=pltpu.VMEM)
SM = pl.BlockSpec(memory_space=pltpu.SMEM)
HB = pl.BlockSpec(memory_space=pltpu.HBM)
GRANT = 119 * 2**19
HEAD = ("y", "x")
CTX = ("z", "core")


def dot(a, b):
    return jnp.dot(a, b, preferred_element_type=F32)


def iota(shape, dim):
    return lax.broadcasted_iota(jnp.int32, shape, dim)


def pack_kernel(q_ref, out_ref):
    shape = (NH * 16, TG * 128)
    r, c = iota(shape, 0), iota(shape, 1)
    head = 8 * (r // 16) + HL * lax.axis_index("core") + r % HL
    pick = ((r // HL) % TG == c // 128) & (head == c % 128)
    pick = jnp.where(pick, 1.0, 0.0).astype(BF)
    rot = []
    for t in range(2):
        x = jnp.concatenate([q_ref[TG * t + i] for i in range(TG)], axis=1)
        y = lax.dot_general(pick, x, (((1,), (1,)), ((), ())), preferred_element_type=F32).astype(BF)
        for j in range(4):
            out_ref[:, 32 * j + 16 * t : 32 * j + 16 * t + 16, :] = y[:, 128 * j : 128 * j + 128].reshape(NH, 16, 128)
        rot.append(y[:, DC:])
    out_ref[:, 128:144, :] = jnp.concatenate(rot, axis=1).reshape(NH, 16, 128)


def pack(q):
    return pl.pallas_call(
        pack_kernel,
        grid=(2,),
        out_shape=jax.ShapeDtypeStruct((NH, QR, 128), BF),
        in_specs=[pl.BlockSpec((2 * TG, WIDE, 128), lambda u: (u, 0, 0))],
        out_specs=pl.BlockSpec((NH, QR // 2, 128), lambda u: (0, u, 0)),
        compiler_params=pltpu.CompilerParams(vmem_limit_bytes=GRANT),
        cost_estimate=pl.CostEstimate(flops=10**9, bytes_accessed=4 * 10**6, transcendentals=0),
    )(q)


def attend_kernel(len0, len1, span_ref, q_ref, w_ref, c0, c1, out_ref, w_scr, c_scr, qr, sco, acc, ml, sem, wsem):
    core, span = lax.axis_index("core"), span_ref[0]
    shard = 2 * lax.axis_index("z") + core
    wcopy = pltpu.make_async_copy(w_ref.at[pl.ds(HL * core, HL)], w_scr, wsem)
    loads = []
    for b in range(2 * NBLK):
        src = (c0, c1)[b // NBLK].at[:, pl.ds(b % NBLK * BLK, BLK)]
        loads.append(pltpu.make_async_copy(src, c_scr.at[b], sem.at[b]))
    loads[0].start()

    for u in range(2):
        for j in range(4):
            line = 144 * u + 32 * j
            qr[:, 32 * u : 32 * u + 32, 128 * j : 128 * j + 128] = q_ref[:, line : line + 32, :]
        rot = q_ref[:, 144 * u + 128 : 144 * u + 144, :]
        qr[:, 32 * u : 32 * u + 16, DC:WIDE] = rot[:, :, 0:DR]
        qr[:, 32 * u + 16 : 32 * u + 32, DC:WIDE] = rot[:, :, DR:]

    token = iota((1, ROWS), 1) // HL
    slot = iota((BLK, ROWS), 0)
    ml[0:1] = jnp.full((1, ROWS), LOW, F32)
    ml[1:2] = jnp.zeros((1, ROWS), F32)
    acc[...] = jnp.zeros_like(acc)

    def score(b, _):
        pltpu.make_async_copy(c0.at[:, pl.ds(0, BLK)], c_scr.at[b], sem.at[b]).wait()

        @pl.when(b == 0)
        def _():
            for c in loads[1:]:
                c.start()
            wcopy.start()

        s = b // NBLK
        filled = jnp.where(s == 0, len0[0], len1[0])
        first = jnp.where(s == 0, shard, shard + 1 - 2 * core) * SLOTS
        limit = jnp.minimum(filled, span + 1 + token - first) - b % NBLK * BLK
        x = lax.dot_general(c_scr[b], qr[...].reshape(ROWS, WIDE), (((0,), (1,)), ((), ())), preferred_element_type=F32)
        x = jnp.where(slot < limit, x, LOW)
        sco[b] = x
        ml[0:1] = jnp.maximum(ml[0:1], jnp.max(x, axis=0, keepdims=True))
        return 0

    def weigh(b, _):
        p = jnp.exp2((sco[b] - ml[0:1]) * SCALE2)
        ml[1:2] = ml[1:2] + jnp.sum(p, axis=0, keepdims=True)
        acc[...] += dot(c_scr[b, 0:DC], p.astype(BF))
        return 0

    lax.fori_loop(0, 2 * NBLK, score, 0, unroll=2)
    lax.fori_loop(0, 2 * NBLK, weigh, 0, unroll=2)

    wcopy.wait()
    total = jnp.maximum(ml[1:2], 1.0)
    lse = ml[0:1] * SCALE2 + jnp.log2(total)
    part = (acc[...] * (1.0 / total)).astype(BF)
    which = iota((1, ROWS), 1) % HL
    res = jnp.zeros((DV, ROWS), F32)
    for h in range(HL):
        up = lax.dot_general(w_scr[h], part, (((0,), (0,)), ((), ())), preferred_element_type=F32)
        res = jnp.where(which == h, up, res)
    out_ref[:, 0:CR, :] = res.T.astype(BF).reshape(NH, CR, DV)
    hi = lse.astype(BF).astype(F32)
    mid = (lse - hi).astype(BF).astype(F32)
    low = lse - hi - mid
    row = iota((16, ROWS), 0)
    tail = jnp.where(row == 0, hi, jnp.where(row == 1, mid, low)).astype(BF)
    for a in range(NX):
        line = a * CR // 128 * 128
        out_ref[a, CR : CR + 16, :] = tail[:, line : line + 128]


def attend(len0, len1, span, q, w, c0, c1):
    return pl.pallas_call(
        attend_kernel,
        out_shape=jax.ShapeDtypeStruct((NX, CR + 16, 128), BF),
        in_specs=[SM, SM, SM, VM, HB, HB, HB],
        out_specs=VM,
        scratch_shapes=[
            pltpu.VMEM((HL, DC, DV), BF),
            pltpu.VMEM((2 * NBLK, WIDE, BLK), BF),
            pltpu.VMEM((NH, CR, WIDE), BF),
            pltpu.VMEM((2 * NBLK, BLK, ROWS), F32),
            pltpu.VMEM((DC, ROWS), F32),
            pltpu.VMEM((8, ROWS), F32),
            pltpu.SemaphoreType.DMA((2 * NBLK,)),
            pltpu.SemaphoreType.DMA,
        ],
        compiler_params=pltpu.CompilerParams(vmem_limit_bytes=44 * 2**20),
        cost_estimate=pl.CostEstimate(flops=10**10, bytes_accessed=6 * 10**6, transcendentals=4 * 10**6),
    )(len0, len1, span, q, w, c0, c1)


def merge_kernel(x_ref, out_ref, scr):
    lines = []
    for k in range(2):
        lse = []
        for z in range(NX // 2):
            t = x_ref[2 * z + k, CR : CR + 16, :].astype(F32)
            lse.append(t[0:1] + t[1:2] + t[2:3])
        lse = jnp.concatenate(lse, axis=0)
        wz = jnp.exp2(lse - jnp.max(lse, axis=0, keepdims=True))
        lines.append(wz / jnp.sum(wz, axis=0, keepdims=True))
    lines.append(jnp.zeros((128 - NX, 128), F32))
    scr[...] = jnp.concatenate(lines, axis=0).T
    off = lax.axis_index("core") * CR
    wt = scr[pl.ds(pl.multiple_of(off, CR), CR), :]
    merged = []
    for k in range(2):
        num = jnp.zeros((CR, DV), F32)
        for z in range(NX // 2):
            at = k * (NX // 2) + z
            num = num + wt[:, at : at + 1] * x_ref[2 * z + k, 0:CR, :].astype(F32)
        merged.append(num.astype(BF))
    merged = jnp.concatenate(merged, axis=0)
    r, c = iota((128, 128), 0), iota((128, 128), 1)
    pick = (r // 8 == c % CR // HL) & (r % 8 == HL * (c // CR) + c % HL)
    out_ref[...] = dot(jnp.where(pick, 1.0, 0.0).astype(BF), merged).astype(BF)


def merge(x):
    return pl.pallas_call(
        merge_kernel,
        out_shape=jax.ShapeDtypeStruct((TOK * 2 * HL, DV), BF),
        in_specs=[VM],
        out_specs=VM,
        scratch_shapes=[pltpu.VMEM((128, 128), F32)],
        compiler_params=pltpu.CompilerParams(vmem_limit_bytes=8 * 2**20),
        cost_estimate=pl.CostEstimate(flops=10**6, bytes_accessed=3 * 10**5, transcendentals=1000),
    )(x)


def body(queries, cache, cache_len, span_start, value_up):
    swap = [(0, 1), (1, 0)]
    mine = cache.T
    other = lax.ppermute(mine, "core", swap)
    other_len = lax.ppermute(cache_len, "core", swap)
    q = lax.all_to_all(pack(queries.transpose(0, 2, 1)), HEAD, split_axis=0, concat_axis=0, tiled=True)
    up = pltpu.with_memory_space_constraint(value_up, pltpu.HBM)
    part = attend(cache_len, other_len, span_start, q, up, mine, other)
    part = lax.all_to_all(part, CTX, split_axis=0, concat_axis=0, tiled=True)
    return merge(part).reshape(TOK, 2 * HL, DV)


def solution(mesh):
    fine = Mesh(mesh.devices.reshape(4, 4, 8, 2), ("y", "x", "z", "core"))
    placed = (P(HEAD, None, None), P(CTX, None), P(CTX), P(), P(HEAD, None, None))
    return jax.shard_map(body, mesh=fine, in_specs=placed, out_specs=P(CTX, HEAD, None), check_vma=False)
```

time: 260 us -> 70.2 us (0.27)
  waiting for transfers between devices: 135 us -> 18.2 us
  matrix products: 29 us -> 0 us
  blocking collectives: 48.8 us -> 22.4 us
  Pallas kernels: 0 us -> 19.4 us
  between operations: 14.8 us -> 1.33 us
  other arithmetic: 12.6 us -> 0 us
  local copies, waits for them, and re-layouts: 10.1 us -> 0.01 us
    reduce_scatter x2 -> x0, waiting for transfers between devices: 97.3 us -> none  [the longest x1 63 us: body(): lax.psum_scatter(scaled[:, :, None] * partial_value.astype(jnp.float32),...]
    pmax x1 -> x0, blocking collectives: 48.8 us -> none  [body(): top = lax.pmax(lse, 'ctx')]
    dot_general x3 -> x0, matrix products: 29 us -> none  [the longest x1 15.9 us: body(): jnp.dot(flat, cache[:, :DC], preferred_element_type=jnp.float32)]
    all_to_all x0 -> x1, blocking collectives: none -> 22.4 us  [body(): part = lax.all_to_all(part, CTX, split_axis=0, concat_axis=0, tiled=True)]
    pallas_call x0 -> x3, Pallas kernels: none -> 19.4 us  [the longest x1 14.5 us: attend(): pl.pallas_call(attend_kernel, out_shape=jax.ShapeDtypeStruct((NX, CR + 16...]
    all_to_all x1, waiting for transfers between devices: 37.2 us -> 18.2 us  [body(): lax.all_to_all(pack(queries.transpose(0, 2, 1)), HEAD, split_axis=0, conc...]
    dot_general x1 -> x0, other arithmetic: 11.5 us -> none  [body(): jnp.dot(flat, cache[:, :DC], preferred_element_type=jnp.float32)]
    unnamed x5 -> x2, local copies, waits for them, and re-layouts: 4.99 us -> 0.01 us
  transfers between devices with their start and end apart: 3 -> 3, of which waited for: 3 -> 1; matrix products, arithmetic and copies ran while one was open for 7% -> 0% of each run, Pallas kernels for 0% -> 5%
where the time goes in v3:
time: 70.2 us; the launch traced here: 70 us
  blocking collectives  22.4 us (32%)
  Pallas kernels  19.4 us (28%)
  waiting for transfers between devices  18.2 us (26%)
  starting transfers between devices  8.63 us (12%)
  between operations  1.33 us (2%)
    all_to_all x1, blocking collectives, body(): part = lax.all_to_all(part, CTX, split_axis=0, concat_axis=0, tiled=True)  22.4 us
    all_to_all x1, waiting for transfers between devices, body(): lax.all_to_all(pack(queries.transpose(0, 2, 1)), HEAD, split_axis=0, conc...  18.2 us
    pallas_call x1, Pallas kernels, attend(): pl.pallas_call(attend_kernel, out_shape=jax.ShapeDtypeStruct((NX, CR + 16...  14.5 us
    all_to_all x1, starting transfers between devices, body(): lax.all_to_all(pack(queries.transpose(0, 2, 1)), HEAD, split_axis=0, conc...  5.02 us
    pallas_call x1, Pallas kernels, pack(): pl.pallas_call(pack_kernel, grid=(2,), out_shape=jax.ShapeDtypeStruct((NH...  3.67 us
    ppermute x1, starting transfers between devices, body(): other = lax.ppermute(mine, 'core', swap)  3.24 us
  transfers between devices with their start and end apart: 3, of which 1 were waited for; matrix products, arithmetic and copies ran while one was open for 0% of the time, Pallas kernels for 5%

profile of v3, /device:TPU:1, one launch (start us, length us, event | category | flops | bytes accessed | tf_op | source)
XLA Modules:
  0.0 70.0 jit_solution(5450636888708708899)
XLA Ops:
  0.0 3.2 %collective-permute-start.1 = (bf16[576,2048]{1,0:T(8,128)(2,1)}, bf16[576,2048]{1,0:T(8,128)(2,1)}, u32[]{:S(2)}, u32[]{:S(2)}) collective-permute-start(bf16[576,2048]{1,0:T(8,128)(2,1)} %bitcast.3), channel_id=1, source_target_pairs={{0,1},{1,0},{2,3},{3,2},{4,5},{5,4},{6,7},{7,6},{8,9},{9,8},{10,11... | collective-permute-start | bytes 7077896 | tf_op jit(solution)/shard_map/ppermute | solution.py:209
  3.2 0.0 copy-start
  3.2 3.7 %shard_map.55 = bf16[16,288,128]{2,1,0:T(8,128)(2,1)} custom-call(bf16[16,576,128]{2,1,0:T(8,128)(2,1)} %bitcast.5), custom_call_target="tpu_custom_call" | custom-call | flops 1000000000 | bytes 4000000 | tf_op jit(solution)/shard_map/pallas_call | solution.py:63
  6.9 5.0 %all-to-all-start = ((bf16[16,288,128]{2,1,0:T(8,128)(2,1)}), bf16[16,288,128]{2,1,0:T(8,128)(2,1)S(1)}, u32[]{:S(2)}, u32[]{:S(2)}) async-start(bf16[16,288,128]{2,1,0:T(8,128)(2,1)} %shard_map.55), calls=%async_computation | async-start | bytes 2359296 | tf_op jit(solution)/shard_map/all_to_all | solution.py:211
  11.9 0.4 collective-permute-start
  13.6 0.0 collective-permute-done.len1
  13.6 18.2 %all-to-all-done.q_ref = bf16[16,288,128]{2,1,0:T(8,128)(2,1)S(1)} async-done(((bf16[16,288,128]{2,1,0:T(8,128)(2,1)}), bf16[16,288,128]{2,1,0:T(8,128)(2,1)S(1)}, u32[]{:S(2)}, u32[]{:S(2)}) %all-to-all-start) | async-done | bytes 1179680 | tf_op jit(solution)/shard_map/all_to_all | solution.py:211
  31.8 0.0 collective-permute-done.1.c1
  31.8 0.0 copy-done
  31.8 14.5 %shard_map.56 = bf16[16,80,128]{2,1,0:T(8,128)(2,1)S(1)} custom-call(s32[1]{0:T(128)S(6)} %copy.6.len0, s32[1]{0:T(128)} %collective-permute-done.len1, s32[1]{0:T(128)S(6)} %copy.7.span_ref, bf16[16,288,128]{2,1,0:T(8,128)(2,1)S(1)} %all-to-all-done.q_ref, bf16[8,512,128]{2,1,0:T(8,128)(2,1)} %w_ref.1, bf16[576,2048]{1,0:T(8,128)(2,1)S(1)} %bitcast.4, ...), custom_call_target="tpu_custom_call" | custom-call | flops 10000000000 | bytes 6000000 | tf_op jit(solution)/shard_map/pallas_call | solution.py:147
  46.4 22.4 %all_to_all.10.x_ref = bf16[16,80,128]{2,1,0:T(8,128)(2,1)S(1)} all-to-all(bf16[16,80,128]{2,1,0:T(8,128)(2,1)S(1)} %shard_map.56), channel_id=1, replica_groups=mesh['y'=4,'x'=4,'z'=8,'core'=2] {'z','core'}, dimensions={0} | all-to-all | bytes 655360 | tf_op jit(solution)/shard_map/all_to_all | solution.py:214
  68.8 1.2 %shard_map.57 = bf16[128,128]{1,0:T(8,128)(2,1)} custom-call(bf16[16,80,128]{2,1,0:T(8,128)(2,1)S(1)} %all_to_all.10.x_ref), custom_call_target="tpu_custom_call" | custom-call | flops 1000000 | bytes 300000 | tf_op jit(solution)/shard_map/pallas_call | solution.py:195
Async XLA Ops:
  0.0 31.8 %collective-permute-start.1 = (bf16[576,2048]{1,0:T(8,128)(2,1)}, bf16[576,2048]{1,0:T(8,128)(2,1)}, u32[]{:S(2)}, u32[]{:S(2)}) collective-permute-start(bf16[576,2048]{1,0:T(8,128)(2,1)} %bitcast.3), channel_id=1, source_target_pairs={{0,1},{1,0},{2,3},{3,2},{4,5},{5,4},{6,7},{7,6},{8,9},{9,8},{10,11... | collective-permute-start | bytes 7077896 | tf_op jit(solution)/shard_map/ppermute | solution.py:209
  3.2 28.6 %copy-start = (bf16[2048,576]{0,1:T(8,128)(2,1)S(1)}, bf16[2048,576]{0,1:T(8,128)(2,1)}, u32[]{:S(2)}) copy-start(bf16[2048,576]{0,1:T(8,128)(2,1)} %param.6) | copy-start | bytes 7077892
  6.9 24.9 %all-to-all-start = ((bf16[16,288,128]{2,1,0:T(8,128)(2,1)}), bf16[16,288,128]{2,1,0:T(8,128)(2,1)S(1)}, u32[]{:S(2)}, u32[]{:S(2)}) async-start(bf16[16,288,128]{2,1,0:T(8,128)(2,1)} %shard_map.55), calls=%async_computation | async-start | bytes 2359296 | tf_op jit(solution)/shard_map/all_to_all | solution.py:211
  11.9 1.7 %collective-permute-start = (s32[1]{0:T(128)}, s32[1]{0:T(128)}, u32[]{:S(2)}, u32[]{:S(2)}) collective-permute-start(s32[1]{0:T(128)} %param.7), channel_id=1, source_target_pairs={{0,1},{1,0},{2,3},{3,2},{4,5},{5,4},{6,7},{7,6},{8,9},{9,8},{10,11... | collective-permute-start | bytes 20 | tf_op jit(solution)/shard_map/ppermute | solution.py:210

commit v4 on v3

--- a/solution.py
+++ b/solution.py
@@ -71,25 +71,51 @@
     )(q)
 
 
-def attend_kernel(len0, len1, span_ref, q_ref, w_ref, c0, c1, out_ref, w_scr, c_scr, qr, sco, acc, ml, sem, wsem):
+def fold_kernel(w_ref, c0, c1, out_ref):
+    core = lax.axis_index("core")
+    w = jnp.concatenate([w_ref[HL * core + h] for h in range(HL)], axis=1)
+    for b in range(2 * NBLK):
+        c = (c0, c1)[b // NBLK][0:DC, b % NBLK * BLK : b % NBLK * BLK + BLK]
+        out_ref[b] = lax.dot_general(w, c, (((0,), (0,)), ((), ())), preferred_element_type=F32).astype(BF)
+
+
+def fold(w, c0, c1):
+    return pl.pallas_call(
+        fold_kernel,
+        out_shape=jax.ShapeDtypeStruct((2 * NBLK, HL * DV, BLK), BF),
+        in_specs=[VM, VM, VM],
+        out_specs=VM,
+        compiler_params=pltpu.CompilerParams(vmem_limit_bytes=44 * 2**20),
+        cost_estimate=pl.CostEstimate(flops=2 * 10**9, bytes_accessed=10**7, transcendentals=0),
+    )(w, c0, c1)
+
+
+def attend_kernel(len0, len1, span_ref, q_ref, u_ref, c0, c1, out_ref, u_scr, c_scr, qr, sco, acc, ml, sem, usem):
     core, span = lax.axis_index("core"), span_ref[0]
     shard = 2 * lax.axis_index("z") + core
-    wcopy = pltpu.make_async_copy(w_ref.at[pl.ds(HL * core, HL)], w_scr, wsem)
     loads = []
     for b in range(2 * NBLK):
         src = (c0, c1)[b // NBLK].at[:, pl.ds(b % NBLK * BLK, BLK)]
         loads.append(pltpu.make_async_copy(src, c_scr.at[b], sem.at[b]))
     loads[0].start()
 
-    for u in range(2):
-        for j in range(4):
-            line = 144 * u + 32 * j
-            qr[:, 32 * u : 32 * u + 32, 128 * j : 128 * j + 128] = q_ref[:, line : line + 32, :]
-        rot = q_ref[:, 144 * u + 128 : 144 * u + 144, :]
-        qr[:, 32 * u : 32 * u + 16, DC:WIDE] = rot[:, :, 0:DR]
-        qr[:, 32 * u + 16 : 32 * u + 32, DC:WIDE] = rot[:, :, DR:]
-
-    token = iota((1, ROWS), 1) // HL
+    r, c = iota((256, 256), 0), iota((256, 256), 1)
+    pick = (r // 64 == c % HL) & (r // 16 % 4 == c // 64) & (r % 16 == c % 64 // HL)
+    pick = jnp.where(pick, 1.0, 0.0).astype(BF)
+    for g in range(NH // 4):
+        x = q_ref[4 * g : 4 * g + 4]
+        parts = [
+            jnp.concatenate([x[:, 32 * j : 32 * j + 32], x[:, 144 + 32 * j : 176 + 32 * j]], axis=1).reshape(256, 128)
+            for j in range(4)
+        ]
+        rot = [x[:, 144 * u + 128 : 144 * u + 144, DR * v : DR * v + DR] for u in range(2) for v in range(2)]
+        parts.append(jnp.concatenate(rot, axis=1).reshape(256, DR))
+        for j, part in enumerate(parts):
+            y = dot(pick, part).astype(BF)
+            for h in range(HL):
+                qr[256 * h + 64 * g : 256 * h + 64 * g + 64, 128 * j : 128 * j + y.shape[1]] = y[64 * h : 64 * h + 64]
+
+    token = iota((1, ROWS), 1) % 256
     slot = iota((BLK, ROWS), 0)
     ml[0:1] = jnp.full((1, ROWS), LOW, F32)
     ml[1:2] = jnp.zeros((1, ROWS), F32)
@@ -102,13 +128,13 @@
         def _():
             for c in loads[1:]:
                 c.start()
-            wcopy.start()
+            pltpu.make_async_copy(u_ref, u_scr, usem).start()
 
         s = b // NBLK
         filled = jnp.where(s == 0, len0[0], len1[0])
         first = jnp.where(s == 0, shard, shard + 1 - 2 * core) * SLOTS
         limit = jnp.minimum(filled, span + 1 + token - first) - b % NBLK * BLK
-        x = lax.dot_general(c_scr[b], qr[...].reshape(ROWS, WIDE), (((0,), (1,)), ((), ())), preferred_element_type=F32)
+        x = lax.dot_general(c_scr[b], qr[...], (((0,), (1,)), ((), ())), preferred_element_type=F32)
         x = jnp.where(slot < limit, x, LOW)
         sco[b] = x
         ml[0:1] = jnp.maximum(ml[0:1], jnp.max(x, axis=0, keepdims=True))
@@ -117,51 +143,49 @@
     def weigh(b, _):
         p = jnp.exp2((sco[b] - ml[0:1]) * SCALE2)
         ml[1:2] = ml[1:2] + jnp.sum(p, axis=0, keepdims=True)
-        acc[...] += dot(c_scr[b, 0:DC], p.astype(BF))
+        p = p.astype(BF)
+        for h in range(HL):
+            acc[:, 256 * h : 256 * h + 256] += dot(u_scr[b, DV * h : DV * h + DV], p[:, 256 * h : 256 * h + 256])
         return 0
 
     lax.fori_loop(0, 2 * NBLK, score, 0, unroll=2)
+    pltpu.make_async_copy(u_ref, u_scr, usem).wait()
     lax.fori_loop(0, 2 * NBLK, weigh, 0, unroll=2)
 
-    wcopy.wait()
     total = jnp.maximum(ml[1:2], 1.0)
     lse = ml[0:1] * SCALE2 + jnp.log2(total)
-    part = (acc[...] * (1.0 / total)).astype(BF)
-    which = iota((1, ROWS), 1) % HL
-    res = jnp.zeros((DV, ROWS), F32)
+    res = (acc[...] * (1.0 / total)).T.astype(BF)
     for h in range(HL):
-        up = lax.dot_general(w_scr[h], part, (((0,), (0,)), ((), ())), preferred_element_type=F32)
-        res = jnp.where(which == h, up, res)
-    out_ref[:, 0:CR, :] = res.T.astype(BF).reshape(NH, CR, DV)
+        out_ref[:, 16 * h : 16 * h + 16, :] = res[256 * h : 256 * h + 256].reshape(NX, 16, DV)
     hi = lse.astype(BF).astype(F32)
     mid = (lse - hi).astype(BF).astype(F32)
     low = lse - hi - mid
-    row = iota((16, ROWS), 0)
-    tail = jnp.where(row == 0, hi, jnp.where(row == 1, mid, low)).astype(BF)
-    for a in range(NX):
-        line = a * CR // 128 * 128
-        out_ref[a, CR : CR + 16, :] = tail[:, line : line + 128]
-
-
-def attend(len0, len1, span, q, w, c0, c1):
+    for line in range(2):
+        tail = [x[:, 256 * h + 128 * line : 256 * h + 128 * line + 128] for x in (hi, mid, low) for h in range(HL)]
+        tail = jnp.concatenate(tail + tail[:4], axis=0).astype(BF)
+        for a in range(8):
+            out_ref[8 * line + a, CR : CR + 16, :] = tail
+
+
+def attend(len0, len1, span, q, u, c0, c1):
     return pl.pallas_call(
         attend_kernel,
         out_shape=jax.ShapeDtypeStruct((NX, CR + 16, 128), BF),
         in_specs=[SM, SM, SM, VM, HB, HB, HB],
         out_specs=VM,
         scratch_shapes=[
-            pltpu.VMEM((HL, DC, DV), BF),
+            pltpu.VMEM((2 * NBLK, HL * DV, BLK), BF),
             pltpu.VMEM((2 * NBLK, WIDE, BLK), BF),
-            pltpu.VMEM((NH, CR, WIDE), BF),
+            pltpu.VMEM((ROWS, WIDE), BF),
             pltpu.VMEM((2 * NBLK, BLK, ROWS), F32),
-            pltpu.VMEM((DC, ROWS), F32),
+            pltpu.VMEM((DV, ROWS), F32),
             pltpu.VMEM((8, ROWS), F32),
             pltpu.SemaphoreType.DMA((2 * NBLK,)),
             pltpu.SemaphoreType.DMA,
         ],
         compiler_params=pltpu.CompilerParams(vmem_limit_bytes=44 * 2**20),
         cost_estimate=pl.CostEstimate(flops=10**10, bytes_accessed=6 * 10**6, transcendentals=4 * 10**6),
-    )(len0, len1, span, q, w, c0, c1)
+    )(len0, len1, span, q, u, c0, c1)
 
 
 def merge_kernel(x_ref, out_ref, scr):
@@ -170,24 +194,28 @@
         lse = []
         for z in range(NX // 2):
             t = x_ref[2 * z + k, CR : CR + 16, :].astype(F32)
-            lse.append(t[0:1] + t[1:2] + t[2:3])
-        lse = jnp.concatenate(lse, axis=0)
-        wz = jnp.exp2(lse - jnp.max(lse, axis=0, keepdims=True))
-        lines.append(wz / jnp.sum(wz, axis=0, keepdims=True))
-    lines.append(jnp.zeros((128 - NX, 128), F32))
+            lse.append(t[0:4] + t[4:8] + t[8:12])
+        top = lse[0]
+        for x in lse[1:]:
+            top = jnp.maximum(top, x)
+        wz = [jnp.exp2(x - top) for x in lse]
+        scale = 1.0 / sum(wz)
+        lines += [x * scale for x in wz]
+    lines.append(jnp.zeros((128 - NX * HL, 128), F32))
     scr[...] = jnp.concatenate(lines, axis=0).T
-    off = lax.axis_index("core") * CR
-    wt = scr[pl.ds(pl.multiple_of(off, CR), CR), :]
+    off = (2 * lax.axis_index("z") + lax.axis_index("core")) % 8 * TOK
+    wt = scr[pl.ds(pl.multiple_of(off, TOK), TOK), :]
     merged = []
     for k in range(2):
-        num = jnp.zeros((CR, DV), F32)
-        for z in range(NX // 2):
-            at = k * (NX // 2) + z
-            num = num + wt[:, at : at + 1] * x_ref[2 * z + k, 0:CR, :].astype(F32)
-        merged.append(num.astype(BF))
+        for h in range(HL):
+            num = jnp.zeros((TOK, DV), F32)
+            for z in range(NX // 2):
+                at = (k * (NX // 2) + z) * HL + h
+                num = num + wt[:, at : at + 1] * x_ref[2 * z + k, 16 * h : 16 * h + 16, :].astype(F32)
+            merged.append(num.astype(BF))
     merged = jnp.concatenate(merged, axis=0)
     r, c = iota((128, 128), 0), iota((128, 128), 1)
-    pick = (r // 8 == c % CR // HL) & (r % 8 == HL * (c // CR) + c % HL)
+    pick = (r // 8 == c % TOK) & (r % 8 == c // TOK)
     out_ref[...] = dot(jnp.where(pick, 1.0, 0.0).astype(BF), merged).astype(BF)
 
 
@@ -209,8 +237,8 @@
     other = lax.ppermute(mine, "core", swap)
     other_len = lax.ppermute(cache_len, "core", swap)
     q = lax.all_to_all(pack(queries.transpose(0, 2, 1)), HEAD, split_axis=0, concat_axis=0, tiled=True)
-    up = pltpu.with_memory_space_constraint(value_up, pltpu.HBM)
-    part = attend(cache_len, other_len, span_start, q, up, mine, other)
+    folded = pltpu.with_memory_space_constraint(fold(value_up, mine, other), pltpu.HBM)
+    part = attend(cache_len, other_len, span_start, q, folded, mine, other)
     part = lax.all_to_all(part, CTX, split_axis=0, concat_axis=0, tiled=True)
     return merge(part).reshape(TOK, 2 * HL, DV)
 

time: 70.2 us -> 68.3 us (0.973)
  waiting for transfers between devices: 18.2 us -> 11 us
  local copies, waits for them, and re-layouts: 0.01 us -> 3.16 us
  Pallas kernels: 19.4 us -> 21.5 us
    all_to_all x1, waiting for transfers between devices: 18.2 us -> 11 us  [body(): lax.all_to_all(pack(queries.transpose(0, 2, 1)), HEAD, split_axis=0, conc...]
    pallas_call x0 -> x1, Pallas kernels: none -> 4.04 us  [fold(): pl.pallas_call(fold_kernel, out_shape=jax.ShapeDtypeStruct((2 * NBLK, HL...]
    unnamed x2 -> x6, local copies, waits for them, and re-layouts: 0.01 us -> 3.16 us
    pallas_call x1, Pallas kernels: 14.5 us -> 12.6 us  [attend(): pl.pallas_call(attend_kernel, out_shape=jax.ShapeDtypeStruct((NX, CR + 16...]
  transfers between devices with their start and end apart: 3 -> 3, of which waited for: 1 -> 1; matrix products, arithmetic and copies ran while one was open for 0% -> 0% of each run, Pallas kernels for 5% -> 11%
where the time goes in v4:
time: 68.3 us; the launch traced here: 68.1 us
  blocking collectives  22.4 us (33%)
  Pallas kernels  21.5 us (31%)
  waiting for transfers between devices  11 us (16%)
  starting transfers between devices  8.63 us (13%)
  local copies, waits for them, and re-layouts  3.16 us (5%)
  between operations  1.36 us (2%)
    all_to_all x1, blocking collectives, body(): part = lax.all_to_all(part, CTX, split_axis=0, concat_axis=0, tiled=True)  22.4 us
    pallas_call x1, Pallas kernels, attend(): pl.pallas_call(attend_kernel, out_shape=jax.ShapeDtypeStruct((NX, CR + 16...  12.6 us
    all_to_all x1, waiting for transfers between devices, body(): lax.all_to_all(pack(queries.transpose(0, 2, 1)), HEAD, split_axis=0, conc...  11 us
    all_to_all x1, starting transfers between devices, body(): lax.all_to_all(pack(queries.transpose(0, 2, 1)), HEAD, split_axis=0, conc...  5.02 us
    pallas_call x1, Pallas kernels, fold(): pl.pallas_call(fold_kernel, out_shape=jax.ShapeDtypeStruct((2 * NBLK, HL...  4.04 us
    pallas_call x1, Pallas kernels, pack(): pl.pallas_call(pack_kernel, grid=(2,), out_shape=jax.ShapeDtypeStruct((NH...  3.64 us
    ppermute x1, starting transfers between devices, body(): other = lax.ppermute(mine, 'core', swap)  3.24 us
    unnamed x6, local copies, waits for them, and re-layouts  3.16 us
  transfers between devices with their start and end apart: 3, of which 1 were waited for; matrix products, arithmetic and copies ran while one was open for 0% of the time, Pallas kernels for 11%

profile of v4, /device:TPU:1, one launch (start us, length us, event | category | flops | bytes accessed | tf_op | source)
XLA Modules:
  0.0 68.1 jit_solution(11137427312543725556)
XLA Ops:
  0.0 3.2 %collective-permute-start.1 = (bf16[576,2048]{1,0:T(8,128)(2,1)}, bf16[576,2048]{1,0:T(8,128)(2,1)}, u32[]{:S(2)}, u32[]{:S(2)}) collective-permute-start(bf16[576,2048]{1,0:T(8,128)(2,1)} %bitcast.3), channel_id=1, source_target_pairs={{0,1},{1,0},{2,3},{3,2},{4,5},{5,4},{6,7},{7,6},{8,9},{9,8},{10,11... | collective-permute-start | bytes 7077896 | tf_op jit(solution)/shard_map/ppermute | solution.py:237
  3.2 0.0 copy-start.1
  3.2 3.6 %shard_map.55 = bf16[16,288,128]{2,1,0:T(8,128)(2,1)} custom-call(bf16[16,576,128]{2,1,0:T(8,128)(2,1)} %bitcast.6), custom_call_target="tpu_custom_call" | custom-call | flops 1000000000 | bytes 4000000 | tf_op jit(solution)/shard_map/pallas_call | solution.py:63
  6.9 5.0 %all-to-all-start = ((bf16[16,288,128]{2,1,0:T(8,128)(2,1)}), bf16[16,288,128]{2,1,0:T(8,128)(2,1)S(1)}, u32[]{:S(2)}, u32[]{:S(2)}) async-start(bf16[16,288,128]{2,1,0:T(8,128)(2,1)} %shard_map.55), calls=%async_computation | async-start | bytes 2359296 | tf_op jit(solution)/shard_map/all_to_all | solution.py:239
  11.9 0.4 collective-permute-start
  13.6 0.0 collective-permute-done.1.c1
  13.6 0.0 copy-done.1
  13.6 0.0 copy-start.2
  13.6 1.2 %copy-done.2 = bf16[8,512,128]{2,1,0:T(8,128)(2,1)S(1)} copy-done((bf16[8,512,128]{2,1,0:T(8,128)(2,1)S(1)}, bf16[8,512,128]{2,1,0:T(8,128)(2,1)}, u32[]{:S(2)}) %copy-start.2) | copy-done | bytes 1048600
  14.8 4.0 %shard_map.56.u_ref = bf16[4,512,1024]{2,1,0:T(8,128)(2,1)S(1)} custom-call(bf16[8,512,128]{2,1,0:T(8,128)(2,1)S(1)} %copy-done.2, bf16[576,2048]{1,0:T(8,128)(2,1)S(1)} %bitcast.4, bf16[576,2048]{1,0:T(8,128)(2,1)} %collective-permute-done.1.c1), custom_call_target="tpu_custom_call" | custom-call | flops 2000000000 | bytes 10000000 | tf_op jit(solution)/shard_map/pallas_call | solution.py:83
  18.9 0.0 copy-start
  18.9 1.9 %copy-done = bf16[4,512,1024]{2,1,0:T(8,128)(2,1)} copy-done((bf16[4,512,1024]{2,1,0:T(8,128)(2,1)}, bf16[4,512,1024]{2,1,0:T(8,128)(2,1)S(1)}, u32[]{:S(2)}) %copy-start) | copy-done | bytes 4194328
  20.8 0.0 collective-permute-done.len1
  20.8 11.0 %all-to-all-done.q_ref = bf16[16,288,128]{2,1,0:T(8,128)(2,1)S(1)} async-done(((bf16[16,288,128]{2,1,0:T(8,128)(2,1)}), bf16[16,288,128]{2,1,0:T(8,128)(2,1)S(1)}, u32[]{:S(2)}, u32[]{:S(2)}) %all-to-all-start) | async-done | bytes 1179680 | tf_op jit(solution)/shard_map/all_to_all | solution.py:239
  31.8 12.6 %shard_map.57 = bf16[16,80,128]{2,1,0:T(8,128)(2,1)S(1)} custom-call(s32[1]{0:T(128)S(6)} %copy.6.len0, s32[1]{0:T(128)} %collective-permute-done.len1, s32[1]{0:T(128)S(6)} %copy.7.span_ref, bf16[16,288,128]{2,1,0:T(8,128)(2,1)S(1)} %all-to-all-done.q_ref, bf16[4,512,1024]{2,1,0:T(8,128)(2,1)} %copy-done, bf16[576,2048]{1,0:T(8,128)(2,1)S(1)} %bitcast.5, ...), custom_call_target="tpu_custom_call" | custom-call | flops 10000000000 | bytes 6000000 | tf_op jit(solution)/shard_map/pallas_call | solution.py:171
  44.4 22.4 %all_to_all.10.x_ref = bf16[16,80,128]{2,1,0:T(8,128)(2,1)S(1)} all-to-all(bf16[16,80,128]{2,1,0:T(8,128)(2,1)S(1)} %shard_map.57), channel_id=1, replica_groups=mesh['y'=4,'x'=4,'z'=8,'core'=2] {'z','core'}, dimensions={0} | all-to-all | bytes 655360 | tf_op jit(solution)/shard_map/all_to_all | solution.py:242
  66.9 1.2 %shard_map.58 = bf16[128,128]{1,0:T(8,128)(2,1)} custom-call(bf16[16,80,128]{2,1,0:T(8,128)(2,1)S(1)} %all_to_all.10.x_ref), custom_call_target="tpu_custom_call" | custom-call | flops 1000000 | bytes 300000 | tf_op jit(solution)/shard_map/pallas_call | solution.py:223
Async XLA Ops:
  0.0 13.6 %collective-permute-start.1 = (bf16[576,2048]{1,0:T(8,128)(2,1)}, bf16[576,2048]{1,0:T(8,128)(2,1)}, u32[]{:S(2)}, u32[]{:S(2)}) collective-permute-start(bf16[576,2048]{1,0:T(8,128)(2,1)} %bitcast.3), channel_id=1, source_target_pairs={{0,1},{1,0},{2,3},{3,2},{4,5},{5,4},{6,7},{7,6},{8,9},{9,8},{10,11... | collective-permute-start | bytes 7077896 | tf_op jit(solution)/shard_map/ppermute | solution.py:237
  3.2 10.4 %copy-start.1 = (bf16[2048,576]{0,1:T(8,128)(2,1)S(1)}, bf16[2048,576]{0,1:T(8,128)(2,1)}, u32[]{:S(2)}) copy-start(bf16[2048,576]{0,1:T(8,128)(2,1)} %param.6) | copy-start | bytes 7077892
  6.9 24.9 %all-to-all-start = ((bf16[16,288,128]{2,1,0:T(8,128)(2,1)}), bf16[16,288,128]{2,1,0:T(8,128)(2,1)S(1)}, u32[]{:S(2)}, u32[]{:S(2)}) async-start(bf16[16,288,128]{2,1,0:T(8,128)(2,1)} %shard_map.55), calls=%async_computation | async-start | bytes 2359296 | tf_op jit(solution)/shard_map/all_to_all | solution.py:239
  11.9 8.9 %collective-permute-start = (s32[1]{0:T(128)}, s32[1]{0:T(128)}, u32[]{:S(2)}, u32[]{:S(2)}) collective-permute-start(s32[1]{0:T(128)} %param.7), channel_id=1, source_target_pairs={{0,1},{1,0},{2,3},{3,2},{4,5},{5,4},{6,7},{7,6},{8,9},{9,8},{10,11... | collective-permute-start | bytes 20 | tf_op jit(solution)/shard_map/ppermute | solution.py:238
  13.6 1.2 %copy-start.2 = (bf16[8,512,128]{2,1,0:T(8,128)(2,1)S(1)}, bf16[8,512,128]{2,1,0:T(8,128)(2,1)}, u32[]{:S(2)}) copy-start(bf16[8,512,128]{2,1,0:T(8,128)(2,1)} %w_ref.1) | copy-start | bytes 3145732
  18.9 1.9 %copy-start = (bf16[4,512,1024]{2,1,0:T(8,128)(2,1)}, bf16[4,512,1024]{2,1,0:T(8,128)(2,1)S(1)}, u32[]{:S(2)}) copy-start(bf16[4,512,1024]{2,1,0:T(8,128)(2,1)S(1)} %shard_map.56.u_ref) | copy-start | bytes 12582916

commit v5 on v4

--- a/solution.py
+++ b/solution.py
@@ -110,10 +110,9 @@
         ]
         rot = [x[:, 144 * u + 128 : 144 * u + 144, DR * v : DR * v + DR] for u in range(2) for v in range(2)]
         parts.append(jnp.concatenate(rot, axis=1).reshape(256, DR))
-        for j, part in enumerate(parts):
-            y = dot(pick, part).astype(BF)
-            for h in range(HL):
-                qr[256 * h + 64 * g : 256 * h + 64 * g + 64, 128 * j : 128 * j + y.shape[1]] = y[64 * h : 64 * h + 64]
+        y = dot(pick, jnp.concatenate(parts, axis=1)).astype(BF)
+        for h in range(HL):
+            qr[256 * h + 64 * g : 256 * h + 64 * g + 64, :] = y[64 * h : 64 * h + 64]
 
     token = iota((1, ROWS), 1) % 256
     slot = iota((BLK, ROWS), 0)
@@ -150,7 +149,7 @@
 
     lax.fori_loop(0, 2 * NBLK, score, 0, unroll=2)
     pltpu.make_async_copy(u_ref, u_scr, usem).wait()
-    lax.fori_loop(0, 2 * NBLK, weigh, 0, unroll=2)
+    lax.fori_loop(0, 2 * NBLK, weigh, 0, unroll=4)
 
     total = jnp.maximum(ml[1:2], 1.0)
     lse = ml[0:1] * SCALE2 + jnp.log2(total)

time: 68.3 us -> 67.8 us (level)
  no operation moved by 1% of the time
where the time goes in v5:
time: 67.8 us; the launch traced here: 67.6 us
  blocking collectives  22.4 us (33%)
  Pallas kernels  21 us (31%)
  waiting for transfers between devices  11 us (16%)
  starting transfers between devices  8.63 us (13%)
  local copies, waits for them, and re-layouts  3.16 us (5%)
  between operations  1.36 us (2%)
    all_to_all x1, blocking collectives, body(): part = lax.all_to_all(part, CTX, split_axis=0, concat_axis=0, tiled=True)  22.4 us
    pallas_call x1, Pallas kernels, attend(): pl.pallas_call(attend_kernel, out_shape=jax.ShapeDtypeStruct((NX, CR + 16...  12.1 us
    all_to_all x1, waiting for transfers between devices, body(): lax.all_to_all(pack(queries.transpose(0, 2, 1)), HEAD, split_axis=0, conc...  11 us
    all_to_all x1, starting transfers between devices, body(): lax.all_to_all(pack(queries.transpose(0, 2, 1)), HEAD, split_axis=0, conc...  5.02 us
    pallas_call x1, Pallas kernels, fold(): pl.pallas_call(fold_kernel, out_shape=jax.ShapeDtypeStruct((2 * NBLK, HL...  4.04 us
    pallas_call x1, Pallas kernels, pack(): pl.pallas_call(pack_kernel, grid=(2,), out_shape=jax.ShapeDtypeStruct((NH...  3.64 us
    ppermute x1, starting transfers between devices, body(): other = lax.ppermute(mine, 'core', swap)  3.24 us
    unnamed x6, local copies, waits for them, and re-layouts  3.16 us
  transfers between devices with their start and end apart: 3, of which 1 were waited for; matrix products, arithmetic and copies ran while one was open for 0% of the time, Pallas kernels for 11%

profile of v5, /device:TPU:1, one launch (start us, length us, event | category | flops | bytes accessed | tf_op | source)
XLA Modules:
  0.0 67.6 jit_solution(14837059193079800805)
XLA Ops:
  0.0 3.2 %collective-permute-start.1 = (bf16[576,2048]{1,0:T(8,128)(2,1)}, bf16[576,2048]{1,0:T(8,128)(2,1)}, u32[]{:S(2)}, u32[]{:S(2)}) collective-permute-start(bf16[576,2048]{1,0:T(8,128)(2,1)} %bitcast.3), channel_id=1, source_target_pairs={{0,1},{1,0},{2,3},{3,2},{4,5},{5,4},{6,7},{7,6},{8,9},{9,8},{10,11... | collective-permute-start | bytes 7077896 | tf_op jit(solution)/shard_map/ppermute | solution.py:236
  3.2 0.0 copy-start.1
  3.2 3.6 %shard_map.55 = bf16[16,288,128]{2,1,0:T(8,128)(2,1)} custom-call(bf16[16,576,128]{2,1,0:T(8,128)(2,1)} %bitcast.6), custom_call_target="tpu_custom_call" | custom-call | flops 1000000000 | bytes 4000000 | tf_op jit(solution)/shard_map/pallas_call | solution.py:63
  6.9 5.0 %all-to-all-start = ((bf16[16,288,128]{2,1,0:T(8,128)(2,1)}), bf16[16,288,128]{2,1,0:T(8,128)(2,1)S(1)}, u32[]{:S(2)}, u32[]{:S(2)}) async-start(bf16[16,288,128]{2,1,0:T(8,128)(2,1)} %shard_map.55), calls=%async_computation | async-start | bytes 2359296 | tf_op jit(solution)/shard_map/all_to_all | solution.py:238
  11.9 0.4 collective-permute-start
  13.6 0.0 collective-permute-done.1.c1
  13.6 0.0 copy-done.1
  13.6 0.0 copy-start.2
  13.6 1.2 %copy-done.2 = bf16[8,512,128]{2,1,0:T(8,128)(2,1)S(1)} copy-done((bf16[8,512,128]{2,1,0:T(8,128)(2,1)S(1)}, bf16[8,512,128]{2,1,0:T(8,128)(2,1)}, u32[]{:S(2)}) %copy-start.2) | copy-done | bytes 1048600
  14.8 4.0 %shard_map.56.u_ref = bf16[4,512,1024]{2,1,0:T(8,128)(2,1)S(1)} custom-call(bf16[8,512,128]{2,1,0:T(8,128)(2,1)S(1)} %copy-done.2, bf16[576,2048]{1,0:T(8,128)(2,1)S(1)} %bitcast.4, bf16[576,2048]{1,0:T(8,128)(2,1)} %collective-permute-done.1.c1), custom_call_target="tpu_custom_call" | custom-call | flops 2000000000 | bytes 10000000 | tf_op jit(solution)/shard_map/pallas_call | solution.py:83
  18.9 0.0 copy-start
  18.9 1.9 %copy-done = bf16[4,512,1024]{2,1,0:T(8,128)(2,1)} copy-done((bf16[4,512,1024]{2,1,0:T(8,128)(2,1)}, bf16[4,512,1024]{2,1,0:T(8,128)(2,1)S(1)}, u32[]{:S(2)}) %copy-start) | copy-done | bytes 4194328
  20.8 0.0 collective-permute-done.len1
  20.8 11.0 %all-to-all-done.q_ref = bf16[16,288,128]{2,1,0:T(8,128)(2,1)S(1)} async-done(((bf16[16,288,128]{2,1,0:T(8,128)(2,1)}), bf16[16,288,128]{2,1,0:T(8,128)(2,1)S(1)}, u32[]{:S(2)}, u32[]{:S(2)}) %all-to-all-start) | async-done | bytes 1179680 | tf_op jit(solution)/shard_map/all_to_all | solution.py:238
  31.8 12.1 %shard_map.57 = bf16[16,80,128]{2,1,0:T(8,128)(2,1)S(1)} custom-call(s32[1]{0:T(128)S(6)} %copy.6.len0, s32[1]{0:T(128)} %collective-permute-done.len1, s32[1]{0:T(128)S(6)} %copy.7.span_ref, bf16[16,288,128]{2,1,0:T(8,128)(2,1)S(1)} %all-to-all-done.q_ref, bf16[4,512,1024]{2,1,0:T(8,128)(2,1)} %copy-done, bf16[576,2048]{1,0:T(8,128)(2,1)S(1)} %bitcast.5, ...), custom_call_target="tpu_custom_call" | custom-call | flops 10000000000 | bytes 6000000 | tf_op jit(solution)/shard_map/pallas_call | solution.py:170
  43.9 22.4 %all_to_all.10.x_ref = bf16[16,80,128]{2,1,0:T(8,128)(2,1)S(1)} all-to-all(bf16[16,80,128]{2,1,0:T(8,128)(2,1)S(1)} %shard_map.57), channel_id=1, replica_groups=mesh['y'=4,'x'=4,'z'=8,'core'=2] {'z','core'}, dimensions={0} | all-to-all | bytes 655360 | tf_op jit(solution)/shard_map/all_to_all | solution.py:241
  66.4 1.2 %shard_map.58 = bf16[128,128]{1,0:T(8,128)(2,1)} custom-call(bf16[16,80,128]{2,1,0:T(8,128)(2,1)S(1)} %all_to_all.10.x_ref), custom_call_target="tpu_custom_call" | custom-call | flops 1000000 | bytes 300000 | tf_op jit(solution)/shard_map/pallas_call | solution.py:222
Async XLA Ops:
  0.0 13.6 %collective-permute-start.1 = (bf16[576,2048]{1,0:T(8,128)(2,1)}, bf16[576,2048]{1,0:T(8,128)(2,1)}, u32[]{:S(2)}, u32[]{:S(2)}) collective-permute-start(bf16[576,2048]{1,0:T(8,128)(2,1)} %bitcast.3), channel_id=1, source_target_pairs={{0,1},{1,0},{2,3},{3,2},{4,5},{5,4},{6,7},{7,6},{8,9},{9,8},{10,11... | collective-permute-start | bytes 7077896 | tf_op jit(solution)/shard_map/ppermute | solution.py:236
  3.2 10.4 %copy-start.1 = (bf16[2048,576]{0,1:T(8,128)(2,1)S(1)}, bf16[2048,576]{0,1:T(8,128)(2,1)}, u32[]{:S(2)}) copy-start(bf16[2048,576]{0,1:T(8,128)(2,1)} %param.6) | copy-start | bytes 7077892
  6.9 24.9 %all-to-all-start = ((bf16[16,288,128]{2,1,0:T(8,128)(2,1)}), bf16[16,288,128]{2,1,0:T(8,128)(2,1)S(1)}, u32[]{:S(2)}, u32[]{:S(2)}) async-start(bf16[16,288,128]{2,1,0:T(8,128)(2,1)} %shard_map.55), calls=%async_computation | async-start | bytes 2359296 | tf_op jit(solution)/shard_map/all_to_all | solution.py:238
  11.9 8.9 %collective-permute-start = (s32[1]{0:T(128)}, s32[1]{0:T(128)}, u32[]{:S(2)}, u32[]{:S(2)}) collective-permute-start(s32[1]{0:T(128)} %param.7), channel_id=1, source_target_pairs={{0,1},{1,0},{2,3},{3,2},{4,5},{5,4},{6,7},{7,6},{8,9},{9,8},{10,11... | collective-permute-start | bytes 20 | tf_op jit(solution)/shard_map/ppermute | solution.py:237
  13.6 1.2 %copy-start.2 = (bf16[8,512,128]{2,1,0:T(8,128)(2,1)S(1)}, bf16[8,512,128]{2,1,0:T(8,128)(2,1)}, u32[]{:S(2)}) copy-start(bf16[8,512,128]{2,1,0:T(8,128)(2,1)} %w_ref.1) | copy-start | bytes 3145732
  18.9 1.9 %copy-start = (bf16[4,512,1024]{2,1,0:T(8,128)(2,1)}, bf16[4,512,1024]{2,1,0:T(8,128)(2,1)S(1)}, u32[]{:S(2)}) copy-start(bf16[4,512,1024]{2,1,0:T(8,128)(2,1)S(1)} %shard_map.56.u_ref) | copy-start | bytes 12582916

commit v6 on v5

--- a/solution.py
+++ b/solution.py
@@ -93,11 +93,10 @@
 def attend_kernel(len0, len1, span_ref, q_ref, u_ref, c0, c1, out_ref, u_scr, c_scr, qr, sco, acc, ml, sem, usem):
     core, span = lax.axis_index("core"), span_ref[0]
     shard = 2 * lax.axis_index("z") + core
-    loads = []
-    for b in range(2 * NBLK):
-        src = (c0, c1)[b // NBLK].at[:, pl.ds(b % NBLK * BLK, BLK)]
-        loads.append(pltpu.make_async_copy(src, c_scr.at[b], sem.at[b]))
-    loads[0].start()
+    loads = [pltpu.make_async_copy(c, c_scr.at[s], sem.at[s]) for s, c in enumerate((c0, c1))]
+    for c in loads:
+        c.start()
+    fetch = pltpu.make_async_copy(u_ref, u_scr, usem)
 
     r, c = iota((256, 256), 0), iota((256, 256), 1)
     pick = (r // 64 == c % HL) & (r // 16 % 4 == c // 64) & (r % 16 == c % 64 // HL)
@@ -115,27 +114,25 @@
             qr[256 * h + 64 * g : 256 * h + 64 * g + 64, :] = y[64 * h : 64 * h + 64]
 
     token = iota((1, ROWS), 1) % 256
-    slot = iota((BLK, ROWS), 0)
+    slot = iota((SLOTS, ROWS), 0)
     ml[0:1] = jnp.full((1, ROWS), LOW, F32)
     ml[1:2] = jnp.zeros((1, ROWS), F32)
     acc[...] = jnp.zeros_like(acc)
 
-    def score(b, _):
-        pltpu.make_async_copy(c0.at[:, pl.ds(0, BLK)], c_scr.at[b], sem.at[b]).wait()
-
-        @pl.when(b == 0)
+    def score(s, _):
+        pltpu.make_async_copy(c0, c_scr.at[s], sem.at[s]).wait()
+
+        @pl.when(s == 0)
         def _():
-            for c in loads[1:]:
-                c.start()
-            pltpu.make_async_copy(u_ref, u_scr, usem).start()
-
-        s = b // NBLK
+            fetch.start()
+
         filled = jnp.where(s == 0, len0[0], len1[0])
         first = jnp.where(s == 0, shard, shard + 1 - 2 * core) * SLOTS
-        limit = jnp.minimum(filled, span + 1 + token - first) - b % NBLK * BLK
-        x = lax.dot_general(c_scr[b], qr[...], (((0,), (1,)), ((), ())), preferred_element_type=F32)
+        limit = jnp.minimum(filled, span + 1 + token - first)
+        x = lax.dot_general(c_scr[s], qr[...], (((0,), (1,)), ((), ())), preferred_element_type=F32)
         x = jnp.where(slot < limit, x, LOW)
-        sco[b] = x
+        for b in range(NBLK):
+            sco[NBLK * s + b] = x[BLK * b : BLK * b + BLK]
         ml[0:1] = jnp.maximum(ml[0:1], jnp.max(x, axis=0, keepdims=True))
         return 0
 
@@ -147,8 +144,8 @@
             acc[:, 256 * h : 256 * h + 256] += dot(u_scr[b, DV * h : DV * h + DV], p[:, 256 * h : 256 * h + 256])
         return 0
 
-    lax.fori_loop(0, 2 * NBLK, score, 0, unroll=2)
-    pltpu.make_async_copy(u_ref, u_scr, usem).wait()
+    lax.fori_loop(0, 2, score, 0)
+    fetch.wait()
     lax.fori_loop(0, 2 * NBLK, weigh, 0, unroll=4)
 
     total = jnp.maximum(ml[1:2], 1.0)
@@ -174,12 +171,12 @@
         out_specs=VM,
         scratch_shapes=[
             pltpu.VMEM((2 * NBLK, HL * DV, BLK), BF),
-            pltpu.VMEM((2 * NBLK, WIDE, BLK), BF),
+            pltpu.VMEM((2, WIDE, SLOTS), BF),
             pltpu.VMEM((ROWS, WIDE), BF),
             pltpu.VMEM((2 * NBLK, BLK, ROWS), F32),
             pltpu.VMEM((DV, ROWS), F32),
             pltpu.VMEM((8, ROWS), F32),
-            pltpu.SemaphoreType.DMA((2 * NBLK,)),
+            pltpu.SemaphoreType.DMA((2,)),
             pltpu.SemaphoreType.DMA,
         ],
         compiler_params=pltpu.CompilerParams(vmem_limit_bytes=44 * 2**20),

time: 67.8 us -> 67.6 us (level)
  no operation moved by 1% of the time
where the time goes in v6:
time: 67.6 us; the launch traced here: 67.3 us
  blocking collectives  22.4 us (33%)
  Pallas kernels  20.7 us (31%)
  waiting for transfers between devices  11 us (16%)
  starting transfers between devices  8.63 us (13%)
  local copies, waits for them, and re-layouts  3.16 us (5%)
  between operations  1.36 us (2%)
    all_to_all x1, blocking collectives, body(): part = lax.all_to_all(part, CTX, split_axis=0, concat_axis=0, tiled=True)  22.4 us
    pallas_call x1, Pallas kernels, attend(): pl.pallas_call(attend_kernel, out_shape=jax.ShapeDtypeStruct((NX, CR + 16...  11.9 us
    all_to_all x1, waiting for transfers between devices, body(): lax.all_to_all(pack(queries.transpose(0, 2, 1)), HEAD, split_axis=0, conc...  11 us
    all_to_all x1, starting transfers between devices, body(): lax.all_to_all(pack(queries.transpose(0, 2, 1)), HEAD, split_axis=0, conc...  5.02 us
    pallas_call x1, Pallas kernels, fold(): pl.pallas_call(fold_kernel, out_shape=jax.ShapeDtypeStruct((2 * NBLK, HL...  4.04 us
    pallas_call x1, Pallas kernels, pack(): pl.pallas_call(pack_kernel, grid=(2,), out_shape=jax.ShapeDtypeStruct((NH...  3.64 us
    ppermute x1, starting transfers between devices, body(): other = lax.ppermute(mine, 'core', swap)  3.24 us
    unnamed x6, local copies, waits for them, and re-layouts  3.16 us
  transfers between devices with their start and end apart: 3, of which 1 were waited for; matrix products, arithmetic and copies ran while one was open for 0% of the time, Pallas kernels for 11%

profile of v6, /device:TPU:1, one launch (start us, length us, event | category | flops | bytes accessed | tf_op | source)
XLA Modules:
  0.0 67.3 jit_solution(3734330265139749865)
XLA Ops:
  0.0 3.2 %collective-permute-start.1 = (bf16[576,2048]{1,0:T(8,128)(2,1)}, bf16[576,2048]{1,0:T(8,128)(2,1)}, u32[]{:S(2)}, u32[]{:S(2)}) collective-permute-start(bf16[576,2048]{1,0:T(8,128)(2,1)} %bitcast.3), channel_id=1, source_target_pairs={{0,1},{1,0},{2,3},{3,2},{4,5},{5,4},{6,7},{7,6},{8,9},{9,8},{10,11... | collective-permute-start | bytes 7077896 | tf_op jit(solution)/shard_map/ppermute | solution.py:233
  3.2 0.0 copy-start.1
  3.2 3.6 %shard_map.55 = bf16[16,288,128]{2,1,0:T(8,128)(2,1)} custom-call(bf16[16,576,128]{2,1,0:T(8,128)(2,1)} %bitcast.6), custom_call_target="tpu_custom_call" | custom-call | flops 1000000000 | bytes 4000000 | tf_op jit(solution)/shard_map/pallas_call | solution.py:63
  6.9 5.0 %all-to-all-start = ((bf16[16,288,128]{2,1,0:T(8,128)(2,1)}), bf16[16,288,128]{2,1,0:T(8,128)(2,1)S(1)}, u32[]{:S(2)}, u32[]{:S(2)}) async-start(bf16[16,288,128]{2,1,0:T(8,128)(2,1)} %shard_map.55), calls=%async_computation | async-start | bytes 2359296 | tf_op jit(solution)/shard_map/all_to_all | solution.py:235
  11.9 0.4 collective-permute-start
  13.6 0.0 collective-permute-done.1.c1
  13.6 0.0 copy-done.1
  13.6 0.0 copy-start.2
  13.6 1.2 %copy-done.2 = bf16[8,512,128]{2,1,0:T(8,128)(2,1)S(1)} copy-done((bf16[8,512,128]{2,1,0:T(8,128)(2,1)S(1)}, bf16[8,512,128]{2,1,0:T(8,128)(2,1)}, u32[]{:S(2)}) %copy-start.2) | copy-done | bytes 1048600
  14.8 4.0 %shard_map.56.u_ref = bf16[4,512,1024]{2,1,0:T(8,128)(2,1)S(1)} custom-call(bf16[8,512,128]{2,1,0:T(8,128)(2,1)S(1)} %copy-done.2, bf16[576,2048]{1,0:T(8,128)(2,1)S(1)} %bitcast.4, bf16[576,2048]{1,0:T(8,128)(2,1)} %collective-permute-done.1.c1), custom_call_target="tpu_custom_call" | custom-call | flops 2000000000 | bytes 10000000 | tf_op jit(solution)/shard_map/pallas_call | solution.py:83
  18.9 0.0 copy-start
  18.9 1.9 %copy-done = bf16[4,512,1024]{2,1,0:T(8,128)(2,1)} copy-done((bf16[4,512,1024]{2,1,0:T(8,128)(2,1)}, bf16[4,512,1024]{2,1,0:T(8,128)(2,1)S(1)}, u32[]{:S(2)}) %copy-start) | copy-done | bytes 4194328
  20.8 0.0 collective-permute-done.len1
  20.8 11.0 %all-to-all-done.q_ref = bf16[16,288,128]{2,1,0:T(8,128)(2,1)S(1)} async-done(((bf16[16,288,128]{2,1,0:T(8,128)(2,1)}), bf16[16,288,128]{2,1,0:T(8,128)(2,1)S(1)}, u32[]{:S(2)}, u32[]{:S(2)}) %all-to-all-start) | async-done | bytes 1179680 | tf_op jit(solution)/shard_map/all_to_all | solution.py:235
  31.8 11.9 %shard_map.57 = bf16[16,80,128]{2,1,0:T(8,128)(2,1)S(1)} custom-call(s32[1]{0:T(128)S(6)} %copy.6.len0, s32[1]{0:T(128)} %collective-permute-done.len1, s32[1]{0:T(128)S(6)} %copy.7.span_ref, bf16[16,288,128]{2,1,0:T(8,128)(2,1)S(1)} %all-to-all-done.q_ref, bf16[4,512,1024]{2,1,0:T(8,128)(2,1)} %copy-done, bf16[576,2048]{1,0:T(8,128)(2,1)S(1)} %bitcast.5, ...), custom_call_target="tpu_custom_call" | custom-call | flops 10000000000 | bytes 6000000 | tf_op jit(solution)/shard_map/pallas_call | solution.py:167
  43.7 22.4 %all_to_all.10.x_ref = bf16[16,80,128]{2,1,0:T(8,128)(2,1)S(1)} all-to-all(bf16[16,80,128]{2,1,0:T(8,128)(2,1)S(1)} %shard_map.57), channel_id=1, replica_groups=mesh['y'=4,'x'=4,'z'=8,'core'=2] {'z','core'}, dimensions={0} | all-to-all | bytes 655360 | tf_op jit(solution)/shard_map/all_to_all | solution.py:238
  66.1 1.2 %shard_map.58 = bf16[128,128]{1,0:T(8,128)(2,1)} custom-call(bf16[16,80,128]{2,1,0:T(8,128)(2,1)S(1)} %all_to_all.10.x_ref), custom_call_target="tpu_custom_call" | custom-call | flops 1000000 | bytes 300000 | tf_op jit(solution)/shard_map/pallas_call | solution.py:219
Async XLA Ops:
  0.0 13.6 %collective-permute-start.1 = (bf16[576,2048]{1,0:T(8,128)(2,1)}, bf16[576,2048]{1,0:T(8,128)(2,1)}, u32[]{:S(2)}, u32[]{:S(2)}) collective-permute-start(bf16[576,2048]{1,0:T(8,128)(2,1)} %bitcast.3), channel_id=1, source_target_pairs={{0,1},{1,0},{2,3},{3,2},{4,5},{5,4},{6,7},{7,6},{8,9},{9,8},{10,11... | collective-permute-start | bytes 7077896 | tf_op jit(solution)/shard_map/ppermute | solution.py:233
  3.2 10.4 %copy-start.1 = (bf16[2048,576]{0,1:T(8,128)(2,1)S(1)}, bf16[2048,576]{0,1:T(8,128)(2,1)}, u32[]{:S(2)}) copy-start(bf16[2048,576]{0,1:T(8,128)(2,1)} %param.6) | copy-start | bytes 7077892
  6.9 24.9 %all-to-all-start = ((bf16[16,288,128]{2,1,0:T(8,128)(2,1)}), bf16[16,288,128]{2,1,0:T(8,128)(2,1)S(1)}, u32[]{:S(2)}, u32[]{:S(2)}) async-start(bf16[16,288,128]{2,1,0:T(8,128)(2,1)} %shard_map.55), calls=%async_computation | async-start | bytes 2359296 | tf_op jit(solution)/shard_map/all_to_all | solution.py:235
  11.9 8.9 %collective-permute-start = (s32[1]{0:T(128)}, s32[1]{0:T(128)}, u32[]{:S(2)}, u32[]{:S(2)}) collective-permute-start(s32[1]{0:T(128)} %param.7), channel_id=1, source_target_pairs={{0,1},{1,0},{2,3},{3,2},{4,5},{5,4},{6,7},{7,6},{8,9},{9,8},{10,11... | collective-permute-start | bytes 20 | tf_op jit(solution)/shard_map/ppermute | solution.py:234
  13.6 1.2 %copy-start.2 = (bf16[8,512,128]{2,1,0:T(8,128)(2,1)S(1)}, bf16[8,512,128]{2,1,0:T(8,128)(2,1)}, u32[]{:S(2)}) copy-start(bf16[8,512,128]{2,1,0:T(8,128)(2,1)} %w_ref.1) | copy-start | bytes 3145732
  18.9 1.9 %copy-start = (bf16[4,512,1024]{2,1,0:T(8,128)(2,1)}, bf16[4,512,1024]{2,1,0:T(8,128)(2,1)S(1)}, u32[]{:S(2)}) copy-start(bf16[4,512,1024]{2,1,0:T(8,128)(2,1)S(1)} %shard_map.56.u_ref) | copy-start | bytes 12582916

commit v7 on v6

--- a/solution.py
+++ b/solution.py
@@ -43,7 +43,7 @@
     return lax.broadcasted_iota(jnp.int32, shape, dim)
 
 
-def pack_kernel(q_ref, out_ref):
+def pack_kernel(q0, q1, out_ref):
     shape = (NH * 16, TG * 128)
     r, c = iota(shape, 0), iota(shape, 1)
     head = 8 * (r // 16) + HL * lax.axis_index("core") + r % HL
@@ -51,7 +51,7 @@
     pick = jnp.where(pick, 1.0, 0.0).astype(BF)
     rot = []
     for t in range(2):
-        x = jnp.concatenate([q_ref[TG * t + i] for i in range(TG)], axis=1)
+        x = jnp.concatenate([(q0, q1)[t][i] for i in range(TG)], axis=1)
         y = lax.dot_general(pick, x, (((1,), (1,)), ((), ())), preferred_element_type=F32).astype(BF)
         for j in range(4):
             out_ref[:, 32 * j + 16 * t : 32 * j + 16 * t + 16, :] = y[:, 128 * j : 128 * j + 128].reshape(NH, 16, 128)
@@ -64,11 +64,11 @@
         pack_kernel,
         grid=(2,),
         out_shape=jax.ShapeDtypeStruct((NH, QR, 128), BF),
-        in_specs=[pl.BlockSpec((2 * TG, WIDE, 128), lambda u: (u, 0, 0))],
+        in_specs=[pl.BlockSpec((TG, WIDE, 128), lambda u: (2 * u, 0, 0)), pl.BlockSpec((TG, WIDE, 128), lambda u: (2 * u + 1, 0, 0))],
         out_specs=pl.BlockSpec((NH, QR // 2, 128), lambda u: (0, u, 0)),
         compiler_params=pltpu.CompilerParams(vmem_limit_bytes=GRANT),
         cost_estimate=pl.CostEstimate(flops=10**9, bytes_accessed=4 * 10**6, transcendentals=0),
-    )(q)
+    )(q, q)
 
 
 def fold_kernel(w_ref, c0, c1, out_ref):

time: 67.6 us -> 67.6 us (level)
  no operation moved by 1% of the time
where the time goes in v7:
time: 67.6 us; the launch traced here: 67.2 us
  blocking collectives  22.5 us (33%)
  Pallas kernels  20.5 us (30%)
  waiting for transfers between devices  10.9 us (16%)
  starting transfers between devices  8.77 us (13%)
  local copies, waits for them, and re-layouts  3.16 us (5%)
  between operations  1.36 us (2%)
    all_to_all x1, blocking collectives, body(): part = lax.all_to_all(part, CTX, split_axis=0, concat_axis=0, tiled=True)  22.5 us
    pallas_call x1, Pallas kernels, attend(): pl.pallas_call(attend_kernel, out_shape=jax.ShapeDtypeStruct((NX, CR + 16...  11.9 us
    all_to_all x1, waiting for transfers between devices, body(): lax.all_to_all(pack(queries.transpose(0, 2, 1)), HEAD, split_axis=0, conc...  10.9 us
    all_to_all x1, starting transfers between devices, body(): lax.all_to_all(pack(queries.transpose(0, 2, 1)), HEAD, split_axis=0, conc...  5.15 us
    pallas_call x1, Pallas kernels, fold(): pl.pallas_call(fold_kernel, out_shape=jax.ShapeDtypeStruct((2 * NBLK, HL...  4.04 us
    pallas_call x1, Pallas kernels, pack(): pl.pallas_call(pack_kernel, grid=(2,), out_shape=jax.ShapeDtypeStruct((NH...  3.47 us
    ppermute x1, starting transfers between devices, body(): other = lax.ppermute(mine, 'core', swap)  3.24 us
    unnamed x6, local copies, waits for them, and re-layouts  3.16 us
  transfers between devices with their start and end apart: 3, of which 1 were waited for; matrix products, arithmetic and copies ran while one was open for 0% of the time, Pallas kernels for 11%

profile of v7, /device:TPU:1, one launch (start us, length us, event | category | flops | bytes accessed | tf_op | source)
XLA Modules:
  0.0 67.2 jit_solution(7531699991557514025)
XLA Ops:
  0.0 3.2 %collective-permute-start.1 = (bf16[576,2048]{1,0:T(8,128)(2,1)}, bf16[576,2048]{1,0:T(8,128)(2,1)}, u32[]{:S(2)}, u32[]{:S(2)}) collective-permute-start(bf16[576,2048]{1,0:T(8,128)(2,1)} %bitcast.3), channel_id=1, source_target_pairs={{0,1},{1,0},{2,3},{3,2},{4,5},{5,4},{6,7},{7,6},{8,9},{9,8},{10,11... | collective-permute-start | bytes 7077896 | tf_op jit(solution)/shard_map/ppermute | solution.py:233
  3.2 3.5 %shard_map.55 = bf16[16,288,128]{2,1,0:T(8,128)(2,1)} custom-call(bf16[16,576,128]{2,1,0:T(8,128)(2,1)} %bitcast.6, bf16[16,576,128]{2,1,0:T(8,128)(2,1)} %bitcast.7), custom_call_target="tpu_custom_call" | custom-call | flops 1000000000 | bytes 4000000 | tf_op jit(solution)/shard_map/pallas_call | solution.py:63
  6.7 0.0 copy-start.1
  6.7 5.2 %all-to-all-start = ((bf16[16,288,128]{2,1,0:T(8,128)(2,1)}), bf16[16,288,128]{2,1,0:T(8,128)(2,1)S(1)}, u32[]{:S(2)}, u32[]{:S(2)}) async-start(bf16[16,288,128]{2,1,0:T(8,128)(2,1)} %shard_map.55), calls=%async_computation | async-start | bytes 2359296 | tf_op jit(solution)/shard_map/all_to_all | solution.py:235
  11.9 0.4 collective-permute-start
  13.6 0.0 collective-permute-done.1.c1
  13.6 0.0 copy-done.1
  13.6 0.0 copy-start.2
  13.6 1.2 %copy-done.2 = bf16[8,512,128]{2,1,0:T(8,128)(2,1)S(1)} copy-done((bf16[8,512,128]{2,1,0:T(8,128)(2,1)S(1)}, bf16[8,512,128]{2,1,0:T(8,128)(2,1)}, u32[]{:S(2)}) %copy-start.2) | copy-done | bytes 1048600
  14.8 4.0 %shard_map.56.u_ref = bf16[4,512,1024]{2,1,0:T(8,128)(2,1)S(1)} custom-call(bf16[8,512,128]{2,1,0:T(8,128)(2,1)S(1)} %copy-done.2, bf16[576,2048]{1,0:T(8,128)(2,1)S(1)} %bitcast.4, bf16[576,2048]{1,0:T(8,128)(2,1)} %collective-permute-done.1.c1), custom_call_target="tpu_custom_call" | custom-call | flops 2000000000 | bytes 10000000 | tf_op jit(solution)/shard_map/pallas_call | solution.py:83
  18.9 0.0 copy-start
  18.9 1.9 %copy-done = bf16[4,512,1024]{2,1,0:T(8,128)(2,1)} copy-done((bf16[4,512,1024]{2,1,0:T(8,128)(2,1)}, bf16[4,512,1024]{2,1,0:T(8,128)(2,1)S(1)}, u32[]{:S(2)}) %copy-start) | copy-done | bytes 4194328
  20.8 0.0 collective-permute-done.len1
  20.8 10.9 %all-to-all-done.q_ref = bf16[16,288,128]{2,1,0:T(8,128)(2,1)S(1)} async-done(((bf16[16,288,128]{2,1,0:T(8,128)(2,1)}), bf16[16,288,128]{2,1,0:T(8,128)(2,1)S(1)}, u32[]{:S(2)}, u32[]{:S(2)}) %all-to-all-start) | async-done | bytes 1179680 | tf_op jit(solution)/shard_map/all_to_all | solution.py:235
  31.7 11.9 %shard_map.57 = bf16[16,80,128]{2,1,0:T(8,128)(2,1)S(1)} custom-call(s32[1]{0:T(128)S(6)} %copy.6.len0, s32[1]{0:T(128)} %collective-permute-done.len1, s32[1]{0:T(128)S(6)} %copy.7.span_ref, bf16[16,288,128]{2,1,0:T(8,128)(2,1)S(1)} %all-to-all-done.q_ref, bf16[4,512,1024]{2,1,0:T(8,128)(2,1)} %copy-done, bf16[576,2048]{1,0:T(8,128)(2,1)S(1)} %bitcast.5, ...), custom_call_target="tpu_custom_call" | custom-call | flops 10000000000 | bytes 6000000 | tf_op jit(solution)/shard_map/pallas_call | solution.py:167
  43.6 22.5 %all_to_all.10.x_ref = bf16[16,80,128]{2,1,0:T(8,128)(2,1)S(1)} all-to-all(bf16[16,80,128]{2,1,0:T(8,128)(2,1)S(1)} %shard_map.57), channel_id=1, replica_groups=mesh['y'=4,'x'=4,'z'=8,'core'=2] {'z','core'}, dimensions={0} | all-to-all | bytes 655360 | tf_op jit(solution)/shard_map/all_to_all | solution.py:238
  66.1 1.2 %shard_map.58 = bf16[128,128]{1,0:T(8,128)(2,1)} custom-call(bf16[16,80,128]{2,1,0:T(8,128)(2,1)S(1)} %all_to_all.10.x_ref), custom_call_target="tpu_custom_call" | custom-call | flops 1000000 | bytes 300000 | tf_op jit(solution)/shard_map/pallas_call | solution.py:219
Async XLA Ops:
  0.0 13.6 %collective-permute-start.1 = (bf16[576,2048]{1,0:T(8,128)(2,1)}, bf16[576,2048]{1,0:T(8,128)(2,1)}, u32[]{:S(2)}, u32[]{:S(2)}) collective-permute-start(bf16[576,2048]{1,0:T(8,128)(2,1)} %bitcast.3), channel_id=1, source_target_pairs={{0,1},{1,0},{2,3},{3,2},{4,5},{5,4},{6,7},{7,6},{8,9},{9,8},{10,11... | collective-permute-start | bytes 7077896 | tf_op jit(solution)/shard_map/ppermute | solution.py:233
  6.7 6.9 %copy-start.1 = (bf16[2048,576]{0,1:T(8,128)(2,1)S(1)}, bf16[2048,576]{0,1:T(8,128)(2,1)}, u32[]{:S(2)}) copy-start(bf16[2048,576]{0,1:T(8,128)(2,1)} %param.6) | copy-start | bytes 7077892
  6.7 25.0 %all-to-all-start = ((bf16[16,288,128]{2,1,0:T(8,128)(2,1)}), bf16[16,288,128]{2,1,0:T(8,128)(2,1)S(1)}, u32[]{:S(2)}, u32[]{:S(2)}) async-start(bf16[16,288,128]{2,1,0:T(8,128)(2,1)} %shard_map.55), calls=%async_computation | async-start | bytes 2359296 | tf_op jit(solution)/shard_map/all_to_all | solution.py:235
  11.9 8.9 %collective-permute-start = (s32[1]{0:T(128)}, s32[1]{0:T(128)}, u32[]{:S(2)}, u32[]{:S(2)}) collective-permute-start(s32[1]{0:T(128)} %param.7), channel_id=1, source_target_pairs={{0,1},{1,0},{2,3},{3,2},{4,5},{5,4},{6,7},{7,6},{8,9},{9,8},{10,11... | collective-permute-start | bytes 20 | tf_op jit(solution)/shard_map/ppermute | solution.py:234
  13.6 1.2 %copy-start.2 = (bf16[8,512,128]{2,1,0:T(8,128)(2,1)S(1)}, bf16[8,512,128]{2,1,0:T(8,128)(2,1)}, u32[]{:S(2)}) copy-start(bf16[8,512,128]{2,1,0:T(8,128)(2,1)} %w_ref.1) | copy-start | bytes 3145732
  18.9 1.9 %copy-start = (bf16[4,512,1024]{2,1,0:T(8,128)(2,1)}, bf16[4,512,1024]{2,1,0:T(8,128)(2,1)S(1)}, u32[]{:S(2)}) copy-start(bf16[4,512,1024]{2,1,0:T(8,128)(2,1)S(1)} %shard_map.56.u_ref) | copy-start | bytes 12582916

commit v8 on v7

--- a/solution.py
+++ b/solution.py
@@ -116,8 +116,6 @@
     token = iota((1, ROWS), 1) % 256
     slot = iota((SLOTS, ROWS), 0)
     ml[0:1] = jnp.full((1, ROWS), LOW, F32)
-    ml[1:2] = jnp.zeros((1, ROWS), F32)
-    acc[...] = jnp.zeros_like(acc)
 
     def score(s, _):
         pltpu.make_async_copy(c0, c_scr.at[s], sem.at[s]).wait()
@@ -136,19 +134,19 @@
         ml[0:1] = jnp.maximum(ml[0:1], jnp.max(x, axis=0, keepdims=True))
         return 0
 
-    def weigh(b, _):
+    lax.fori_loop(0, 2, score, 0)
+    fetch.wait()
+    total = 0.0
+    for b in range(2 * NBLK):
         p = jnp.exp2((sco[b] - ml[0:1]) * SCALE2)
-        ml[1:2] = ml[1:2] + jnp.sum(p, axis=0, keepdims=True)
+        total = total + jnp.sum(p, axis=0, keepdims=True)
         p = p.astype(BF)
         for h in range(HL):
-            acc[:, 256 * h : 256 * h + 256] += dot(u_scr[b, DV * h : DV * h + DV], p[:, 256 * h : 256 * h + 256])
-        return 0
-
-    lax.fori_loop(0, 2, score, 0)
-    fetch.wait()
-    lax.fori_loop(0, 2 * NBLK, weigh, 0, unroll=4)
-
-    total = jnp.maximum(ml[1:2], 1.0)
+            cols = slice(256 * h, 256 * h + 256)
+            up = dot(u_scr[b, DV * h : DV * h + DV], p[:, cols])
+            acc[:, cols] = up if b == 0 else acc[:, cols] + up
+
+    total = jnp.maximum(total, 1.0)
     lse = ml[0:1] * SCALE2 + jnp.log2(total)
     res = (acc[...] * (1.0 / total)).T.astype(BF)
     for h in range(HL):

time: 67.6 us -> 67.5 us (level)
  no operation moved by 1% of the time
where the time goes in v8:
time: 67.5 us; the launch traced here: 67.2 us
  blocking collectives  22.5 us (33%)
  Pallas kernels  20.5 us (30%)
  waiting for transfers between devices  10.9 us (16%)
  starting transfers between devices  8.77 us (13%)
  local copies, waits for them, and re-layouts  3.16 us (5%)
  between operations  1.36 us (2%)
    all_to_all x1, blocking collectives, body(): part = lax.all_to_all(part, CTX, split_axis=0, concat_axis=0, tiled=True)  22.5 us
    pallas_call x1, Pallas kernels, attend(): pl.pallas_call(attend_kernel, out_shape=jax.ShapeDtypeStruct((NX, CR + 16...  11.8 us
    all_to_all x1, waiting for transfers between devices, body(): lax.all_to_all(pack(queries.transpose(0, 2, 1)), HEAD, split_axis=0, conc...  10.9 us
    all_to_all x1, starting transfers between devices, body(): lax.all_to_all(pack(queries.transpose(0, 2, 1)), HEAD, split_axis=0, conc...  5.15 us
    pallas_call x1, Pallas kernels, fold(): pl.pallas_call(fold_kernel, out_shape=jax.ShapeDtypeStruct((2 * NBLK, HL...  4.04 us
    pallas_call x1, Pallas kernels, pack(): pl.pallas_call(pack_kernel, grid=(2,), out_shape=jax.ShapeDtypeStruct((NH...  3.47 us
    ppermute x1, starting transfers between devices, body(): other = lax.ppermute(mine, 'core', swap)  3.24 us
    unnamed x6, local copies, waits for them, and re-layouts  3.16 us
  transfers between devices with their start and end apart: 3, of which 1 were waited for; matrix products, arithmetic and copies ran while one was open for 0% of the time, Pallas kernels for 11%

profile of v8, /device:TPU:1, one launch (start us, length us, event | category | flops | bytes accessed | tf_op | source)
XLA Modules:
  0.0 67.2 jit_solution(17987532278139737385)
XLA Ops:
  0.0 3.2 %collective-permute-start.1 = (bf16[576,2048]{1,0:T(8,128)(2,1)}, bf16[576,2048]{1,0:T(8,128)(2,1)}, u32[]{:S(2)}, u32[]{:S(2)}) collective-permute-start(bf16[576,2048]{1,0:T(8,128)(2,1)} %bitcast.3), channel_id=1, source_target_pairs={{0,1},{1,0},{2,3},{3,2},{4,5},{5,4},{6,7},{7,6},{8,9},{9,8},{10,11... | collective-permute-start | bytes 7077896 | tf_op jit(solution)/shard_map/ppermute | solution.py:231
  3.2 3.5 %shard_map.55 = bf16[16,288,128]{2,1,0:T(8,128)(2,1)} custom-call(bf16[16,576,128]{2,1,0:T(8,128)(2,1)} %bitcast.6, bf16[16,576,128]{2,1,0:T(8,128)(2,1)} %bitcast.7), custom_call_target="tpu_custom_call" | custom-call | flops 1000000000 | bytes 4000000 | tf_op jit(solution)/shard_map/pallas_call | solution.py:63
  6.7 0.0 copy-start.1
  6.7 5.2 %all-to-all-start = ((bf16[16,288,128]{2,1,0:T(8,128)(2,1)}), bf16[16,288,128]{2,1,0:T(8,128)(2,1)S(1)}, u32[]{:S(2)}, u32[]{:S(2)}) async-start(bf16[16,288,128]{2,1,0:T(8,128)(2,1)} %shard_map.55), calls=%async_computation | async-start | bytes 2359296 | tf_op jit(solution)/shard_map/all_to_all | solution.py:233
  11.9 0.4 collective-permute-start
  13.6 0.0 collective-permute-done.1.c1
  13.6 0.0 copy-done.1
  13.6 0.0 copy-start.2
  13.6 1.2 %copy-done.2 = bf16[8,512,128]{2,1,0:T(8,128)(2,1)S(1)} copy-done((bf16[8,512,128]{2,1,0:T(8,128)(2,1)S(1)}, bf16[8,512,128]{2,1,0:T(8,128)(2,1)}, u32[]{:S(2)}) %copy-start.2) | copy-done | bytes 1048600
  14.8 4.0 %shard_map.56.u_ref = bf16[4,512,1024]{2,1,0:T(8,128)(2,1)S(1)} custom-call(bf16[8,512,128]{2,1,0:T(8,128)(2,1)S(1)} %copy-done.2, bf16[576,2048]{1,0:T(8,128)(2,1)S(1)} %bitcast.4, bf16[576,2048]{1,0:T(8,128)(2,1)} %collective-permute-done.1.c1), custom_call_target="tpu_custom_call" | custom-call | flops 2000000000 | bytes 10000000 | tf_op jit(solution)/shard_map/pallas_call | solution.py:83
  18.9 0.0 copy-start
  18.9 1.9 %copy-done = bf16[4,512,1024]{2,1,0:T(8,128)(2,1)} copy-done((bf16[4,512,1024]{2,1,0:T(8,128)(2,1)}, bf16[4,512,1024]{2,1,0:T(8,128)(2,1)S(1)}, u32[]{:S(2)}) %copy-start) | copy-done | bytes 4194328
  20.8 0.0 collective-permute-done.len1
  20.8 10.9 %all-to-all-done.q_ref = bf16[16,288,128]{2,1,0:T(8,128)(2,1)S(1)} async-done(((bf16[16,288,128]{2,1,0:T(8,128)(2,1)}), bf16[16,288,128]{2,1,0:T(8,128)(2,1)S(1)}, u32[]{:S(2)}, u32[]{:S(2)}) %all-to-all-start) | async-done | bytes 1179680 | tf_op jit(solution)/shard_map/all_to_all | solution.py:233
  31.7 11.8 %shard_map.57 = bf16[16,80,128]{2,1,0:T(8,128)(2,1)S(1)} custom-call(s32[1]{0:T(128)S(6)} %copy.6.len0, s32[1]{0:T(128)} %collective-permute-done.len1, s32[1]{0:T(128)S(6)} %copy.7.span_ref, bf16[16,288,128]{2,1,0:T(8,128)(2,1)S(1)} %all-to-all-done.q_ref, bf16[4,512,1024]{2,1,0:T(8,128)(2,1)} %copy-done, bf16[576,2048]{1,0:T(8,128)(2,1)S(1)} %bitcast.5, ...), custom_call_target="tpu_custom_call" | custom-call | flops 10000000000 | bytes 6000000 | tf_op jit(solution)/shard_map/pallas_call | solution.py:165
  43.6 22.5 %all_to_all.10.x_ref = bf16[16,80,128]{2,1,0:T(8,128)(2,1)S(1)} all-to-all(bf16[16,80,128]{2,1,0:T(8,128)(2,1)S(1)} %shard_map.57), channel_id=1, replica_groups=mesh['y'=4,'x'=4,'z'=8,'core'=2] {'z','core'}, dimensions={0} | all-to-all | bytes 655360 | tf_op jit(solution)/shard_map/all_to_all | solution.py:236
  66.1 1.2 %shard_map.58 = bf16[128,128]{1,0:T(8,128)(2,1)} custom-call(bf16[16,80,128]{2,1,0:T(8,128)(2,1)S(1)} %all_to_all.10.x_ref), custom_call_target="tpu_custom_call" | custom-call | flops 1000000 | bytes 300000 | tf_op jit(solution)/shard_map/pallas_call | solution.py:217
Async XLA Ops:
  0.0 13.6 %collective-permute-start.1 = (bf16[576,2048]{1,0:T(8,128)(2,1)}, bf16[576,2048]{1,0:T(8,128)(2,1)}, u32[]{:S(2)}, u32[]{:S(2)}) collective-permute-start(bf16[576,2048]{1,0:T(8,128)(2,1)} %bitcast.3), channel_id=1, source_target_pairs={{0,1},{1,0},{2,3},{3,2},{4,5},{5,4},{6,7},{7,6},{8,9},{9,8},{10,11... | collective-permute-start | bytes 7077896 | tf_op jit(solution)/shard_map/ppermute | solution.py:231
  6.7 6.9 %copy-start.1 = (bf16[2048,576]{0,1:T(8,128)(2,1)S(1)}, bf16[2048,576]{0,1:T(8,128)(2,1)}, u32[]{:S(2)}) copy-start(bf16[2048,576]{0,1:T(8,128)(2,1)} %param.6) | copy-start | bytes 7077892
  6.7 25.0 %all-to-all-start = ((bf16[16,288,128]{2,1,0:T(8,128)(2,1)}), bf16[16,288,128]{2,1,0:T(8,128)(2,1)S(1)}, u32[]{:S(2)}, u32[]{:S(2)}) async-start(bf16[16,288,128]{2,1,0:T(8,128)(2,1)} %shard_map.55), calls=%async_computation | async-start | bytes 2359296 | tf_op jit(solution)/shard_map/all_to_all | solution.py:233
  11.9 8.9 %collective-permute-start = (s32[1]{0:T(128)}, s32[1]{0:T(128)}, u32[]{:S(2)}, u32[]{:S(2)}) collective-permute-start(s32[1]{0:T(128)} %param.7), channel_id=1, source_target_pairs={{0,1},{1,0},{2,3},{3,2},{4,5},{5,4},{6,7},{7,6},{8,9},{9,8},{10,11... | collective-permute-start | bytes 20 | tf_op jit(solution)/shard_map/ppermute | solution.py:232
  13.6 1.2 %copy-start.2 = (bf16[8,512,128]{2,1,0:T(8,128)(2,1)S(1)}, bf16[8,512,128]{2,1,0:T(8,128)(2,1)}, u32[]{:S(2)}) copy-start(bf16[8,512,128]{2,1,0:T(8,128)(2,1)} %w_ref.1) | copy-start | bytes 3145732
  18.9 1.9 %copy-start = (bf16[4,512,1024]{2,1,0:T(8,128)(2,1)}, bf16[4,512,1024]{2,1,0:T(8,128)(2,1)S(1)}, u32[]{:S(2)}) copy-start(bf16[4,512,1024]{2,1,0:T(8,128)(2,1)S(1)} %shard_map.56.u_ref) | copy-start | bytes 12582916
